TPU v7x, 128 devices: a whole 4x4x4 slice. The times are simulated.
128 devices in a mesh: lat: 8 (over z, y_lo), lon: 16 (over y_hi, x, core).
Axes of the slice: x: 4, y: 4 (y_hi: 2, y_lo: 2; y = y_hi * 2 + y_lo), z: 4, core: 2. Of those that a mesh axis runs over, the one named last changes fastest.
Arguments:
- tokens: float32 [2, 96, 576, 512], P(None, 'lat', 'lon'), may hold values from -6 to 6
- cotangent: float32 [2, 96, 576, 512], P(None, 'lat', 'lon'), may hold values from -6 to 6
- region_ids: int32 [2, 96, 576], P(None, 'lat', 'lon'), may hold values from 0 to 11, as said below
- w_qkv: bfloat16 [512, 1536], replicated, may hold values from -2 to 2
- w_proj: bfloat16 [512, 512], replicated, may hold values from -0.25 to 0.25
- w_in: bfloat16 [512, 2048], replicated, may hold values from -0.25 to 0.25
- w_out: bfloat16 [2048, 512], replicated, may hold values from -0.125 to 0.125
Outputs:
- grad_tokens: float32 [2, 96, 576, 512], P(None, 'lat', 'lon')
- grad_qkv: float32 [512, 1536], replicated
- grad_proj: float32 [512, 512], replicated
- grad_in: float32 [512, 2048], replicated
- grad_out: float32 [2048, 512], replicated
Inputs may be any that keep to these rules, and one draw needn't show every extreme that they name: `region_ids`: a cell attends only to cells of its window with the same region id; ids are constant on contiguous strips of the shifted grid, changing where the roll wrapped over the band's latitude ends or over the levels, and at one column inside each block of 12 columns.
All inputs are finite; a program needn't handle non-finite values.
Results may differ from a plain program's by a relative error of at most 0.0152.
Values may be sent and summed in bfloat16 or wider, within the bound.
A program may use at most 192 MiB of HBM per device.

v0:
```python
import jax
import jax.numpy as jnp
from jax import lax
from jax.sharding import PartitionSpec as P

HEADS = 16
WLEV = 2
WLAT = 6
WLON = 12


EPS = 1e-05
MASKED = -1000000000.0


def passed_along(value, axis, steps):
    count = lax.axis_size(axis)
    pairs = [(source, (source + steps) % count) for source in range(count)]
    return lax.ppermute(value, axis, pairs)


def norm_rows(values):
    centred = values - jnp.mean(values, axis=-1, keepdims=True)
    spread = jnp.mean(centred * centred, axis=-1, keepdims=True)
    return centred * lax.rsqrt(spread + EPS)


def outer_sum(left_m, right_m):
    return lax.dot_general(
        left_m, right_m, (((0,), (0,)), ((), ())), preferred_element_type=jnp.float32
    )


def times_transposed(left_m, right_m):
    return lax.dot_general(
        left_m, right_m, (((1,), (1,)), ((), ())), preferred_element_type=jnp.float32
    )


def split_windows(lattice):
    levels, rows_lat, cols_lon, channels = lattice.shape
    blocks = lattice.reshape(levels, rows_lat // WLAT, WLAT, cols_lon // WLON, WLON, channels)
    blocks = blocks.transpose(1, 3, 0, 2, 4, 5)
    return blocks.reshape(-1, levels * WLAT * WLON, channels)


def merge_windows(blocks, rows_lat, cols_lon):
    channels = blocks.shape[-1]
    lattice = blocks.reshape(rows_lat // WLAT, cols_lon // WLON, WLEV, WLAT, WLON, channels)
    return lattice.transpose(2, 0, 3, 1, 4, 5).reshape(WLEV, rows_lat, cols_lon, channels)


def core_forward(packed, region):
    win_count, win_size, triple = packed.shape
    features = triple // 3
    head_dim = features // HEADS
    heads_all = packed.reshape(win_count, win_size, 3, HEADS, head_dim)
    queries = heads_all[:, :, 0]
    keys_all = heads_all[:, :, 1]
    values_all = heads_all[:, :, 2]
    scores = jnp.einsum(
        "wqhd,wkhd->whqk", queries, keys_all, preferred_element_type=jnp.float32
    ) * head_dim ** (-0.5)
    allowed = region[:, None, :, None] == region[:, None, None, :]
    scores = jnp.where(allowed, scores, MASKED)
    soft = jax.nn.softmax(scores, axis=-1)
    attn_probs = soft.astype(jnp.bfloat16)
    mixed_heads = jnp.einsum(
        "whqk,wkhd->wqhd", attn_probs, values_all, preferred_element_type=jnp.float32
    )
    mixed_heads = mixed_heads.reshape(win_count, win_size, features).astype(jnp.bfloat16)
    return (mixed_heads, (queries, keys_all, values_all, soft, attn_probs, allowed))


def core_backward(saved, d_mixed):
    queries, keys_all, values_all, soft, attn_probs, allowed = saved
    win_count, win_size, heads_n, head_dim = queries.shape
    d_heads = d_mixed.reshape(win_count, win_size, heads_n, head_dim)
    d_probs = jnp.einsum("wqhd,wkhd->whqk", d_heads, values_all, preferred_element_type=jnp.float32)
    d_probs = d_probs.astype(jnp.bfloat16).astype(jnp.float32)
    d_values = jnp.einsum(
        "whqk,wqhd->wkhd", attn_probs, d_heads, preferred_element_type=jnp.float32
    )
    total = jnp.sum(d_probs * soft, axis=-1, keepdims=True)
    d_scores = jnp.where(allowed, soft * (d_probs - total), 0.0) * head_dim ** (-0.5)
    d_scores = d_scores.astype(jnp.bfloat16)
    d_queries = jnp.einsum(
        "whqk,wkhd->wqhd", d_scores, keys_all, preferred_element_type=jnp.float32
    )
    d_keys = jnp.einsum("whqk,wqhd->wkhd", d_scores, queries, preferred_element_type=jnp.float32)
    d_packed = jnp.stack([d_queries, d_keys, d_values], axis=2)
    return d_packed.reshape(win_count, win_size, -1).astype(jnp.bfloat16)


def attention_forward(normed, region_grid, w_qkv, w_proj):
    rows_lat, cols_lon = (normed.shape[1], normed.shape[2])
    win_in = split_windows(normed)
    region = split_windows(region_grid[..., None])[..., 0]
    flat_in = win_in.reshape(-1, win_in.shape[-1])
    packed = jnp.dot(flat_in, w_qkv, preferred_element_type=jnp.float32).astype(jnp.bfloat16)
    packed = packed.reshape(win_in.shape[0], win_in.shape[1], -1)
    mixed_heads, saved = core_forward(packed, region)
    flat_mixed = mixed_heads.reshape(-1, mixed_heads.shape[-1])
    attended = jnp.dot(flat_mixed, w_proj, preferred_element_type=jnp.float32).astype(jnp.bfloat16)
    attended = merge_windows(attended.reshape(mixed_heads.shape), rows_lat, cols_lon)
    return (attended, (flat_in, packed.shape, flat_mixed, saved))


def attention_backward(kept_attn, d_attended, w_qkv, w_proj):
    flat_in, packed_shape, flat_mixed, saved = kept_attn
    rows_lat, cols_lon = (d_attended.shape[1], d_attended.shape[2])
    d_flat = split_windows(d_attended).reshape(flat_mixed.shape)
    grad_proj = outer_sum(flat_mixed, d_flat)
    d_mixed = times_transposed(d_flat, w_proj).astype(jnp.bfloat16)
    d_packed = core_backward(saved, d_mixed)
    flat_packed = d_packed.reshape(-1, d_packed.shape[-1])
    grad_qkv = outer_sum(flat_in, flat_packed)
    d_normed = times_transposed(flat_packed, w_qkv)
    d_normed = merge_windows(
        d_normed.reshape(packed_shape[0], packed_shape[1], -1), rows_lat, cols_lon
    )
    return (d_normed, grad_qkv, grad_proj)


def mlp_backward(middle, cot_rows, w_in, w_out):
    normed_mid, norm_back = jax.vjp(norm_rows, middle)
    normed_half = normed_mid.astype(jnp.bfloat16)
    pre_act = jnp.dot(normed_half, w_in, preferred_element_type=jnp.float32)
    activated, gelu_back = jax.vjp(jax.nn.gelu, pre_act)
    activated = activated.astype(jnp.bfloat16)
    cot_half = cot_rows.astype(jnp.bfloat16)
    grad_out = outer_sum(activated, cot_half)
    d_act = times_transposed(cot_half, w_out)
    d_pre = gelu_back(d_act)[0].astype(jnp.bfloat16)
    grad_in = outer_sum(normed_half, d_pre)
    d_normed = times_transposed(d_pre, w_in)
    d_mid = cot_rows + norm_back(d_normed)[0]
    return (d_mid, grad_in, grad_out)


def advance(tile_in, axis_pos, half_n, mover):
    length = tile_in.shape[axis_pos]
    leading = lax.slice_in_dim(tile_in, 0, half_n, axis=axis_pos)
    remain = lax.slice_in_dim(tile_in, half_n, length, axis=axis_pos)
    return jnp.concatenate([remain, mover(leading)], axis=axis_pos)


def retreat(tile_in, axis_pos, half_n, mover):
    length = tile_in.shape[axis_pos]
    trailing = lax.slice_in_dim(tile_in, length - half_n, length, axis=axis_pos)
    remain = lax.slice_in_dim(tile_in, 0, length - half_n, axis=axis_pos)
    return jnp.concatenate([mover(trailing), remain], axis=axis_pos)


def shift_ahead(tile_in, lat_mover, lon_mover):
    level_axis = tile_in.ndim - 4
    rolled = jnp.roll(tile_in, -(WLEV // 2), axis=level_axis)
    rolled = advance(rolled, level_axis + 1, WLAT // 2, lat_mover)
    return advance(rolled, level_axis + 2, WLON // 2, lon_mover)


def shift_behind(tile_in, lat_mover, lon_mover):
    level_axis = tile_in.ndim - 4
    rolled = retreat(tile_in, level_axis + 2, WLON // 2, lon_mover)
    rolled = retreat(rolled, level_axis + 1, WLAT // 2, lat_mover)
    return jnp.roll(rolled, WLEV // 2, axis=level_axis)


def strip_lat_ahead(pieces):
    return passed_along(pieces, "lat", -1)


def strip_lon_ahead(pieces):
    return passed_along(pieces, "lon", -1)


def strip_lat_behind(pieces):
    return passed_along(pieces, "lat", 1)


def strip_lon_behind(pieces):
    return passed_along(pieces, "lon", 1)


def grad_lat_behind(pieces):
    return passed_along(pieces.astype(jnp.bfloat16), "lat", 1).astype(pieces.dtype)


def grad_lon_behind(pieces):
    return passed_along(pieces.astype(jnp.bfloat16), "lon", 1).astype(pieces.dtype)


def local(tokens, cotangent, region_ids, w_qkv, w_proj, w_in, w_out):
    features = tokens.shape[-1]
    frame_tokens, frame_cot = (tokens, cotangent)
    normed_full, norm_back = jax.vjp(norm_rows, tokens)
    moved = shift_ahead(normed_full.astype(jnp.bfloat16), strip_lat_ahead, strip_lon_ahead)
    attended, kept_attn = attention_forward(moved, region_ids, w_qkv, w_proj)
    attended = shift_behind(attended, strip_lat_behind, strip_lon_behind)
    middle = frame_tokens + attended.astype(jnp.float32)
    d_mid, grad_in, grad_out = mlp_backward(
        middle.reshape(-1, features), frame_cot.reshape(-1, features), w_in, w_out
    )
    d_mid = d_mid.reshape(middle.shape)
    d_attended = d_mid.astype(jnp.bfloat16)
    d_attended = shift_ahead(d_attended, strip_lat_ahead, strip_lon_ahead)
    d_normed, grad_qkv, grad_proj = attention_backward(kept_attn, d_attended, w_qkv, w_proj)
    d_normed = shift_behind(d_normed, grad_lat_behind, grad_lon_behind)
    d_tokens = d_mid + norm_back(d_normed)[0]
    gradients = (grad_qkv, grad_proj, grad_in, grad_out)
    gradients = lax.psum((grad_qkv, grad_proj, grad_in, grad_out), ("lat", "lon"))
    return (d_tokens, gradients[0], gradients[1], gradients[2], gradients[3])


def solution(mesh):
    in_specs = (
        P(None, "lat", "lon", None),
        P(None, "lat", "lon", None),
        P(None, "lat", "lon"),
        P(),
        P(),
        P(),
        P(),
    )
    out_specs = (P(None, "lat", "lon", None), P(), P(), P(), P())
    return jax.shard_map(local, mesh=mesh, in_specs=in_specs, out_specs=out_specs, check_vma=False)
```

profile of v0, /device:TPU:1, one launch (start us, length us, event | category | flops | bytes accessed | tf_op | source)
XLA Modules:
  0.0 435.0 jit_solution(1698935722339327437)
XLA Ops:
  13.8 5.6 %collective-permute-start = (bf16[2,3,36,512]{3,2,1,0:T(8,128)(2,1)}, bf16[2,3,36,512]{3,2,1,0:T(8,128)(2,1)S(1)}, u32[]{:S(2)}, u32[]{:S(2)}) collective-permute-start(bf16[2,3,36,512]{3,2,1,0:T(8,128)(2,1)} %pad_maximum_fusion.6), channel_id=1, source_target_pairs={{0,112},{16,0},{32,16},{48,32},{64,48},{80,64},{96,80},{112,96},{1... | collective-permute-start | bytes 663560 | tf_op jit(solution)/shard_map/ppermute | solution.py:19
  19.6 4.7 %collective-permute-done = bf16[2,3,36,512]{3,2,1,0:T(8,128)(2,1)S(1)} collective-permute-done((bf16[2,3,36,512]{3,2,1,0:T(8,128)(2,1)}, bf16[2,3,36,512]{3,2,1,0:T(8,128)(2,1)S(1)}, u32[]{:S(2)}, u32[]{:S(2)}) %collective-permute-start) | collective-permute-done | bytes 221216 | tf_op jit(solution)/shard_map/ppermute | solution.py:19
  26.4 4.0 collective-permute-done.1
  32.8 4.7 %convolution_convert_fusion.1 = bf16[864,1536]{1,0:T(8,128)(2,1)} fusion(bf16[864,512]{1,0:T(8,128)(2,1)} %reshape_reshape.13, bf16[512,1536]{1,0:T(8,128)(2,1)} %param.10), kind=kOutput, calls=%fused_computation.36 | convolution fusion | flops 1360281600 | bytes 5111808 | tf_op jit(solution)/shard_map/dot_general | solution.py:100
  37.5 4.9 %copy.156 = bf16[864,1536]{0,1:T(8,128)(2,1)} copy(bf16[864,1536]{1,0:T(8,128)(2,1)} %convolution_convert_fusion.1) | data formatting | bytes 5308416 | tf_op jit(solution)/shard_map/convert_element_type | solution.py:100
  42.4 10.2 %reshape_reshape.14 = bf16[6,144,3,16,32]{1,0,4,3,2:T(8,128)(2,1)} reshape(bf16[864,1536]{0,1:T(8,128)(2,1)} %copy.156) | data formatting | bytes 5308416 | tf_op jit(solution)/shard_map/reshape;reshape | solution.py:57
  52.6 5.8 %fusion.70 = (bf16[6,144,1,16,32]{1,0,4,3,2:T(8,128)(2,1)}, bf16[6,144,1,16,32]{1,0,4,3,2:T(8,128)(2,1)}, bf16[6,144,1,16,32]{1,0,4,3,2:T(8,128)(2,1)}) fusion(bf16[6,144,3,16,32]{1,0,4,3,2:T(8,128)(2,1)} %reshape_reshape.14), kind=kLoop, calls=%fused_computation.122 | loop fusion | bytes 5308416 | tf_op jit(solution)/shard_map/slice | solution.py:59
  58.4 12.9 %fusion.75 = (f32[6,16,144]{2,1,0:T(8,128)S(1)}, f32[6,16,144,144]{2,3,1,0:T(8,128)}) fusion(pred[6,144,144]{1,2,0:T(8,128)(4,1)S(1)} %broadcast_compare_fusion, bf16[6,144,1,16,32]{1,0,4,3,2:T(8,128)(2,1)} %get-tuple-element.39, bf16[6,144,1,16,32]{1,0,4,3,2:T(8,128)(2,1)} %get-tuple-element.38), kind=kOutput, calls=%fused_computation.127 | convolution fusion | flops 135364752 | bytes 9911808 | tf_op jit(solution)/shard_map/sub | solution.py:66
  71.3 6.9 %fusion.37 = bf16[6,144,16,32]{1,3,2,0:T(8,128)(2,1)S(1)} fusion(bf16[6,144,1,16,32]{1,0,4,3,2:T(8,128)(2,1)} %get-tuple-element.40, f32[6,16,144,144]{2,3,1,0:T(8,128)} %get-tuple-element.50, f32[6,16,144]{2,1,0:T(8,128)S(1)} %get-tuple-element.49), kind=kOutput, calls=%fused_computation.63 | convolution fusion | flops 131825664 | bytes 9787392 | tf_op jit(solution)/shard_map/whqk,wkhd->wqhd/dot_general | solution.py:68
  80.7 3.2 convert_element_type.85
  98.5 4.4 %collective-permute-done.3 = bf16[2,3,36,512]{3,0,2,1:T(2,128)(2,1)S(1)} collective-permute-done((bf16[2,3,36,512]{3,0,2,1:T(2,128)(2,1)}, bf16[2,3,36,512]{3,0,2,1:T(2,128)(2,1)S(1)}, u32[]{:S(2)}, u32[]{:S(2)}) %collective-permute-start.3) | collective-permute-done | bytes 221216 | tf_op jit(solution)/shard_map/ppermute | solution.py:19
  105.6 3.5 fusion.69
  109.4 2.8 multiply_reduce_fusion.3
  116.8 3.7 fusion.67
  120.6 6.1 %fusion.16 = bf16[864,2048]{1,0:T(8,128)(2,1)S(1)} fusion(f32[864,2048]{1,0:T(8,128)S(1)} %fusion.67, bf16[2048,512]{1,0:T(8,128)(2,1)S(1)} %copy-done.31, f32[864,512]{1,0:T(8,128)S(1)} %copy-done.11), kind=kOutput, calls=%fused_computation.22 | convolution fusion | flops 1847771136 | bytes 14483456 | tf_op jit(solution)/shard_map/dot_general | solution.py:35
  134.6 8.4 %fusion.26 = f32[2048,512]{1,0:T(8,128)} fusion(f32[864,2048]{1,0:T(8,128)} %copy-done.34, f32[864,512]{1,0:T(8,128)S(1)} %copy-done.12), kind=kOutput, calls=%fused_computation.35 | convolution fusion | flops 1828306944 | bytes 13041664 | tf_op jit(solution)/shard_map/dot_general | solution.py:29
  143.2 8.4 %collective-permute-start.5 = (bf16[2,12,6,512]{3,2,1,0:T(8,128)(2,1)S(1)}, bf16[2,12,6,512]{3,2,1,0:T(8,128)(2,1)S(1)}, u32[]{:S(2)}, u32[]{:S(2)}) collective-permute-start(bf16[2,12,6,512]{3,2,1,0:T(8,128)(2,1)S(1)} %pad_maximum_fusion.8), channel_id=1, source_target_pairs={{0,15},{1,0},{2,1},{3,2},{4,3},{5,4},{6,5},{7,6},{8,7},{9,8},{10,9... | collective-permute-start | bytes 442376 | tf_op jit(solution)/shard_map/ppermute | solution.py:19
  151.5 4.5 %fusion.66 = f32[512,2048]{1,0:T(8,128)} fusion(bf16[864,2048]{1,0:T(8,128)(2,1)S(1)} %copy-done.17, f32[864,512]{1,0:T(8,128)S(1)} %copy-done.9, f32[864]{0:T(1024)S(1)} %rsqrt.21, f32[864]{0:T(1024)S(1)} %div.51), kind=kOutput, calls=%fused_computation.118 | convolution fusion | flops 1813266432 | bytes 9509632 | tf_op jit(solution)/shard_map/dot_general | solution.py:29
  164.1 8.7 %fusion.28 = bf16[6,144,1,16,32]{1,4,3,0,2:T(8,128)(2,1)} fusion(bf16[6,144,16,32]{1,0,3,2:T(8,128)(2,1)S(1)} %reshape.136, f32[6,16,144,144]{2,3,1,0:T(8,128)} %get-tuple-element.50, f32[6,16,144]{2,1,0:T(8,128)S(1)} %copy-done.36), kind=kOutput, calls=%fused_computation.49 | convolution fusion | flops 131383296 | bytes 9787392 | tf_op jit(solution)/shard_map/whqk,wqhd->wkhd/dot_general | solution.py:81
  172.8 5.0 %convolution_convert_fusion = bf16[6,16,144,144]{2,3,1,0:T(8,128)(2,1)} fusion(bf16[6,144,1,16,32]{1,0,4,3,2:T(8,128)(2,1)S(1)} %copy-done.13, bf16[6,144,16,32]{1,0,3,2:T(8,128)(2,1)S(1)} %reshape.136), kind=kOutput, calls=%fused_computation.30 | convolution fusion | flops 129392640 | bytes 5750784 | tf_op jit(solution)/shard_map/wqhd,wkhd->whqk/dot_general | solution.py:79
  177.8 18.5 %fusion.31 = bf16[6,144,1,16,32]{1,4,3,0,2:T(8,128)(2,1)} fusion(bf16[6,16,144,144]{2,3,1,0:T(8,128)(2,1)} %convolution_convert_fusion, pred[6,144,144]{1,2,0:T(8,128)(4,1)S(1)} %broadcast_compare_fusion, bf16[6,144,1,16,32]{1,0,4,3,2:T(8,128)(2,1)} %get-tuple-element.38, f32[6,16,144,144]{2,3,1,0:T(8,128)} %get-tuple-element.50, ...), kind=kOutput, calls=%fused_computation.50 | convolution fusion | flops 147322512 | bytes 13893120 | tf_op jit(solution)/shard_map/whqk,wkhd->wqhd/dot_general | solution.py:87
  196.3 20.5 %fusion.32 = bf16[6,144,1,16,32]{1,4,3,0,2:T(8,128)(2,1)} fusion(bf16[6,16,144,144]{2,3,1,0:T(8,128)(2,1)} %convolution_convert_fusion, pred[6,144,144]{1,2,0:T(8,128)(4,1)S(1)} %broadcast_compare_fusion, bf16[6,144,1,16,32]{1,0,4,3,2:T(8,128)(2,1)S(1)} %copy-done.18, f32[6,16,144,144]{2,3,1,0:T(8,128)} %get-tuple-element.50, f32[6,16,144]{2,1,0:T(8,128)S(1)} %copy-done.36), kind=kOutput, calls=%fused_computation.51 | convolution fusion | flops 147322512 | bytes 13893120 | tf_op jit(solution)/shard_map/whqk,wqhd->wkhd/dot_general | solution.py:90
  216.8 3.0 maximum_convert_fusion
  222.0 8.5 %copy.186 = bf16[6,144,3,16,32]{1,0,4,3,2:T(8,128)(2,1)} copy(bf16[6,144,3,16,32]{1,4,3,0,2:T(8,128)(2,1)S(1)} %maximum_convert_fusion) | data formatting | bytes 5308416 | tf_op jit(solution)/shard_map/convert_element_type | solution.py:92
  230.5 9.4 %convert_element_type.99 = bf16[864,1536]{0,1:T(8,128)(2,1)} reshape(bf16[6,144,3,16,32]{1,0,4,3,2:T(8,128)(2,1)} %copy.186) | data formatting | bytes 5308416 | tf_op jit(solution)/shard_map/convert_element_type | solution.py:92
  239.9 5.3 %fusion.76 = f32[512,1536]{1,0:T(8,128)} fusion(bf16[864,512]{1,0:T(8,128)(2,1)S(1)} %copy-done.23, bf16[864,1536]{0,1:T(8,128)(2,1)} %convert_element_type.99), kind=kOutput, calls=%fused_computation.128 | convolution fusion | flops 1358954496 | bytes 6684672 | tf_op jit(solution)/shard_map/dot_general | solution.py:29
  245.2 12.1 %copy.178 = bf16[6,144,3,16,32]{4,3,2,1,0:T(8,128)(2,1)} copy(bf16[6,144,3,16,32]{1,4,3,0,2:T(8,128)(2,1)} %copy-done.5) | data formatting | bytes 5308416 | tf_op jit(solution)/shard_map/convert_element_type | solution.py:92
  257.3 14.8 %convert_element_type.96 = bf16[2,3,2,6,12,1536]{5,4,3,2,1,0:T(8,128)(2,1)} reshape(bf16[6,144,3,16,32]{4,3,2,1,0:T(8,128)(2,1)} %copy.178) | data formatting | bytes 5308416 | tf_op jit(solution)/shard_map/convert_element_type | solution.py:92
  272.1 4.2 convolution_bitcast_fusion
  281.0 8.0 %collective-permute-done.7 = bf16[2,3,36,512]{3,2,1,0:T(8,128)(2,1)S(1)} collective-permute-done((bf16[2,3,36,512]{3,2,1,0:T(8,128)(2,1)S(1)}, bf16[2,3,36,512]{3,2,1,0:T(8,128)(2,1)S(1)}, u32[]{:S(2)}, u32[]{:S(2)}) %collective-permute-start.7) | collective-permute-done | bytes 221216 | tf_op jit(solution)/shard_map/ppermute | solution.py:19
  296.7 119.6 %all-reduce.3.cloned.1.call-done = (f32[512,1536]{1,0:T(8,128)}, f32[512,512]{1,0:T(8,128)}, f32[512,2048]{1,0:T(8,128)}, f32[2048,512]{1,0:T(8,128)}) async-done(((f32[512,1536]{1,0:T(8,128)}, f32[512,512]{1,0:T(8,128)}, f32[512,2048]{1,0:T(8,128)}, f32[2048,512]{1,0:T(8,128)}), (f32[512,1536]{1,0:T(8,128)}, f32[512,512]{1,0:T(8,128)}, f32[512,2048]{1,0:T(8,128)}, ...) | async-done | bytes 12582928 | tf_op jit(solution)/shard_map/psum | solution.py:211
  416.2 3.9 copy.254
  (165 shorter events, 73.7 us)
Async XLA Ops:
  7.2 109.7 %copy-start = (bf16[512,2048]{1,0:T(8,128)(2,1)S(1)}, bf16[512,2048]{1,0:T(8,128)(2,1)}, u32[]{:S(2)}) copy-start(bf16[512,2048]{1,0:T(8,128)(2,1)} %param.12) | copy-start | bytes 6291460
  7.2 409.1 %all-reduce.3.cloned.1.call-start = ((), (), s32[]{:S(2)}) async-start(), calls=%async_computation | async-start | bytes 25165824 | tf_op jit(solution)/shard_map/psum | solution.py:211
  9.6 2.8 copy-start.24
  9.6 2.8 copy-start.2
  12.8 6.5 %copy-start.30 = (s32[2,12,36]{2,0,1:T(2,128)S(1)}, s32[2,12,36]{2,0,1:T(2,128)}, u32[]{:S(2)}) copy-start(s32[2,12,36]{2,0,1:T(2,128)} %param.9) | copy-start | bytes 10372
  13.8 10.5 %collective-permute-start = (bf16[2,3,36,512]{3,2,1,0:T(8,128)(2,1)}, bf16[2,3,36,512]{3,2,1,0:T(8,128)(2,1)S(1)}, u32[]{:S(2)}, u32[]{:S(2)}) collective-permute-start(bf16[2,3,36,512]{3,2,1,0:T(8,128)(2,1)} %pad_maximum_fusion.6), channel_id=1, source_target_pairs={{0,112},{16,0},{32,16},{48,32},{64,48},{80,64},{96,80},{112,96},{1... | collective-permute-start | bytes 663560 | tf_op jit(solution)/shard_map/ppermute | solution.py:19
  24.3 6.1 %collective-permute-start.1 = (bf16[2,12,6,512]{3,2,1,0:T(8,128)(2,1)S(1)}, bf16[2,12,6,512]{3,2,1,0:T(8,128)(2,1)S(1)}, u32[]{:S(2)}, u32[]{:S(2)}) collective-permute-start(bf16[2,12,6,512]{3,2,1,0:T(8,128)(2,1)S(1)} %pad_maximum_fusion.9), channel_id=1, source_target_pairs={{0,15},{1,0},{2,1},{3,2},{4,3},{5,4},{6,5},{7,6},{8,7},{9,8},{10,9... | collective-permute-start | bytes 442376 | tf_op jit(solution)/shard_map/ppermute | solution.py:19
  71.3 7.0 %copy-start.35 = (f32[6,16,144]{2,1,0:T(8,128)}, f32[6,16,144]{2,1,0:T(8,128)S(1)}, u32[]{:S(2)}) copy-start(f32[6,16,144]{2,1,0:T(8,128)S(1)} %get-tuple-element.49) | copy-start | bytes 165892
  88.8 5.4 %copy-start.19 = (f32[2,12,36,512]{3,0,2,1:T(2,128)S(1)}, f32[2,12,36,512]{3,0,2,1:T(2,128)}, u32[]{:S(2)}) copy-start(f32[2,12,36,512]{3,0,2,1:T(2,128)} %param.8) | copy-start | bytes 5308420
  89.8 3.3 collective-permute-start.2
  94.1 8.7 %collective-permute-start.3 = (bf16[2,3,36,512]{3,0,2,1:T(2,128)(2,1)}, bf16[2,3,36,512]{3,0,2,1:T(2,128)(2,1)S(1)}, u32[]{:S(2)}, u32[]{:S(2)}) collective-permute-start(bf16[2,3,36,512]{3,0,2,1:T(2,128)(2,1)} %pad_maximum_fusion.7), channel_id=1, source_target_pairs={{0,16},{16,32},{32,48},{48,64},{64,80},{80,96},{96,112},{112,0},{1... | collective-permute-start | bytes 663560 | tf_op jit(solution)/shard_map/ppermute | solution.py:19
  109.4 2.8 copy-start.10
  116.8 3.7 copy-start.11
  116.8 3.7 copy-start.31
  120.5 6.1 %copy-start.34 = (f32[864,2048]{1,0:T(8,128)}, f32[864,2048]{1,0:T(8,128)S(1)}, u32[]{:S(2)}) copy-start(f32[864,2048]{1,0:T(8,128)S(1)} %fusion.67) | copy-start | bytes 21233668
  120.5 6.1 %copy-start.8 = (f32[864,512]{1,0:T(8,128)S(1)}, f32[864,512]{1,0:T(8,128)}, u32[]{:S(2)}) copy-start(f32[864,512]{1,0:T(8,128)} %reshape.133) | copy-start | bytes 5308420
  133.8 9.4 %collective-permute-start.4 = (bf16[2,3,36,512]{3,2,1,0:T(8,128)(2,1)S(1)}, bf16[2,3,36,512]{3,2,1,0:T(8,128)(2,1)S(1)}, u32[]{:S(2)}, u32[]{:S(2)}) collective-permute-start(bf16[2,3,36,512]{3,2,1,0:T(8,128)(2,1)S(1)} %pad_maximum_fusion.5), channel_id=1, source_target_pairs={{0,112},{16,0},{32,16},{48,32},{64,48},{80,64},{96,80},{112,96},{1... | collective-permute-start | bytes 663560 | tf_op jit(solution)/shard_map/ppermute | solution.py:19
  134.6 16.9 %copy-start.17 = (bf16[864,2048]{1,0:T(8,128)(2,1)S(1)}, bf16[864,2048]{1,0:T(8,128)(2,1)}, u32[]{:S(2)}) copy-start(bf16[864,2048]{1,0:T(8,128)(2,1)} %copy-done.16) | copy-start | bytes 10616836
  143.0 8.5 %copy-start.9 = (f32[864,512]{1,0:T(8,128)S(1)}, f32[864,512]{1,0:T(8,128)}, u32[]{:S(2)}) copy-start(f32[864,512]{1,0:T(8,128)} %reshape.133) | copy-start | bytes 5308420
  143.2 13.2 %collective-permute-start.5 = (bf16[2,12,6,512]{3,2,1,0:T(8,128)(2,1)S(1)}, bf16[2,12,6,512]{3,2,1,0:T(8,128)(2,1)S(1)}, u32[]{:S(2)}, u32[]{:S(2)}) collective-permute-start(bf16[2,12,6,512]{3,2,1,0:T(8,128)(2,1)S(1)} %pad_maximum_fusion.8), channel_id=1, source_target_pairs={{0,15},{1,0},{2,1},{3,2},{4,3},{5,4},{6,5},{7,6},{8,7},{9,8},{10,9... | collective-permute-start | bytes 442376 | tf_op jit(solution)/shard_map/ppermute | solution.py:19
  160.9 3.1 copy-start.36
  164.1 8.7 %copy-start.13 = (bf16[6,144,1,16,32]{1,0,4,3,2:T(8,128)(2,1)S(1)}, bf16[6,144,1,16,32]{1,0,4,3,2:T(8,128)(2,1)}, u32[]{:S(2)}) copy-start(bf16[6,144,1,16,32]{1,0,4,3,2:T(8,128)(2,1)} %get-tuple-element.40) | copy-start | bytes 2654212
  177.8 18.5 %copy-start.18 = (bf16[6,144,1,16,32]{1,0,4,3,2:T(8,128)(2,1)S(1)}, bf16[6,144,1,16,32]{1,0,4,3,2:T(8,128)(2,1)}, u32[]{:S(2)}) copy-start(bf16[6,144,1,16,32]{1,0,4,3,2:T(8,128)(2,1)} %get-tuple-element.39) | copy-start | bytes 2654212
  219.8 2.1 copy-start.5
  230.5 9.4 %copy-start.23 = (bf16[864,512]{1,0:T(8,128)(2,1)S(1)}, bf16[864,512]{1,0:T(8,128)(2,1)}, u32[]{:S(2)}) copy-start(bf16[864,512]{1,0:T(8,128)(2,1)} %reshape_reshape.13) | copy-start | bytes 2654212
  257.3 14.8 %copy-start.32 = (bf16[512,1536]{1,0:T(8,128)(2,1)S(1)}, bf16[512,1536]{1,0:T(8,128)(2,1)}, u32[]{:S(2)}) copy-start(bf16[512,1536]{1,0:T(8,128)(2,1)} %param.10) | copy-start | bytes 4718596
  277.9 2.9 collective-permute-start.6
  280.9 8.1 %collective-permute-start.7 = (bf16[2,3,36,512]{3,2,1,0:T(8,128)(2,1)S(1)}, bf16[2,3,36,512]{3,2,1,0:T(8,128)(2,1)S(1)}, u32[]{:S(2)}, u32[]{:S(2)}) collective-permute-start(bf16[2,3,36,512]{3,2,1,0:T(8,128)(2,1)S(1)} %fusion.49), channel_id=1, source_target_pairs={{0,16},{16,32},{32,48},{48,64},{64,80},{80,96},{96,112},{112,0},{1... | collective-permute-start | bytes 663560 | tf_op jit(solution)/shard_map/ppermute | solution.py:19
  416.2 3.9 copy-start.20
  416.2 4.9 %copy-start.15 = (f32[512,2048]{1,0:T(8,128)S(1)}, f32[512,2048]{1,0:T(8,128)}, u32[]{:S(2)}) copy-start(f32[512,2048]{1,0:T(8,128)} %get-tuple-element.56) | copy-start | bytes 12582916
  421.1 3.7 copy-start.14
  424.8 3.1 copy-start.1
  (14 other events, 20.5 us)
Sparse Core Ops, SparseCore 0:
  245.3 170.8 all-reduce.2
where the time goes:
time: 441 us; the launch traced here: 435 us
  waiting for transfers between devices  145 us (33%)
  local copies, waits for them, and re-layouts  118 us (27%)
  matrix products  117 us (27%)
  other arithmetic  23.8 us (5%)
  starting transfers between devices  16.3 us (4%)
  between operations  15.1 us (3%)
    psum x1, waiting for transfers between devices, local(): lax.psum((grad_qkv, grad_proj, grad_in, grad_out), ('lat', 'lon'))  120 us
    convert_element_type x4, local copies, waits for them, and re-layouts, core_backward(): return d_packed.reshape(win_count, win_size, -1).astype(jnp.bfloat16)  44.8 us
    ppermute x8, waiting for transfers between devices, passed_along(): return lax.ppermute(value, axis, pairs)  25.7 us
    unnamed x81, local copies, waits for them, and re-layouts  24 us
    dot_general x1, matrix products, core_backward(): jnp.einsum('whqk,wqhd->wkhd', d_scores, queries, preferred_element_type=j...  20.5 us
    dot_general x4, matrix products, outer_sum(): lax.dot_general(left_m, right_m, (((0,), (0,)), ((), ())), preferred_elem...  19.9 us
    dot_general x1, matrix products, core_backward(): jnp.einsum('whqk,wkhd->wqhd', d_scores, keys_all, preferred_element_type=...  18.5 us
    ppermute x8, starting transfers between devices, passed_along(): return lax.ppermute(value, axis, pairs)  16.3 us
  transfers between devices with their start and end apart: 9, of which 7 were waited for; matrix products, arithmetic and copies ran while one was open for 13% of the time, Pallas kernels for 0%

commit v1 on v0

v1 whole, which is shorter than its diff:
```python
import functools

import jax
import jax.numpy as jnp
from jax import lax
from jax.experimental import pallas as pl
from jax.experimental.pallas import tpu as pltpu
from jax.sharding import PartitionSpec as P

D = 512
HEADS = 16
HEAD_DIM = D // HEADS
FFN = 2048
WLEV = 2
WLAT = 6
WLON = 12
WIN = WLEV * WLAT * WLON
GROUP = 8
LANES = GROUP * HEAD_DIM
GROUPS = HEADS // GROUP
SPREAD = GROUP * WIN
HALF_LAT = WLAT // 2
HALF_LON = WLON // 2
EPS = 1e-05
MASKED = -1e10
SCALE = HEAD_DIM ** -0.5
LOG2E = 1.4426950408889634
GELU_A = 0.7978845608028654
GELU_B = 0.044715
F32 = jnp.float32
BF16 = jnp.bfloat16


def nn(a, b):
    return lax.dot_general(a, b, (((1,), (0,)), ((), ())), preferred_element_type=F32)


def nt(a, b):
    return lax.dot_general(a, b, (((1,), (1,)), ((), ())), preferred_element_type=F32)


def norm_parts(v):
    centred = v - jnp.mean(v, axis=-1, keepdims=True)
    r = lax.rsqrt(jnp.mean(centred * centred, axis=-1, keepdims=True) + EPS)
    return centred * r, r


def norm_back(unit, r, g):
    return r * (g - jnp.mean(g, axis=-1, keepdims=True) - unit * jnp.mean(g * unit, axis=-1, keepdims=True))


def spread_heads(v):
    lane_head = lax.broadcasted_iota(jnp.int32, v.shape, 1) // HEAD_DIM
    zero = jnp.zeros_like(v)
    return jnp.concatenate([jnp.where(lane_head == h, v, zero) for h in range(GROUP)], axis=0)


def own_blocks(full):
    return jnp.concatenate(
        [full[HEAD_DIM * h : HEAD_DIM * (h + 1), WIN * h : WIN * (h + 1)] for h in range(GROUP)], axis=0
    )


BLOCKS = 12
OUT_BLOCKS = (0, 2, 4, 6)
IN_BLOCKS = (1, 3, 5, 7)
PROJ_BLOCK = 8
QKV_BLOCKS = (9, 10, 11)
ROUTES = (
    ("xyz", 1), ("yzx", 1), ("zxy", 1), ("xyz", 3), ("yzx", 3), ("zxy", 3),
    ("xyz", 1), ("yzx", 1), ("zxy", 1),
    ("xyz", 0), ("yzx", 0), ("zxy", 0),
)
SLOTS = 17


class Place:
    def __init__(self):
        lat, lon = lax.axis_index("lat"), lax.axis_index("lon")
        self.core = lon % 2
        self.at = {"x": (lon // 2) % 4, "y": (lon // 8) * 2 + lat % 2, "z": lat // 2}

    def mesh_id(self, at, core):
        return (at["z"] * 2 + at["y"] % 2, (at["y"] // 2) * 8 + at["x"] * 2 + core)

    def sibling(self):
        return self.mesh_id(self.at, 1 - self.core)

    def along(self, axis, step):
        at = dict(self.at)
        at[axis] = (at[axis] + step) % 4
        return self.mesh_id(at, self.core), at[axis]

    def across(self, axis, kind):
        at, c = dict(self.at), self.at[axis]
        at[axis] = c + 1 - 2 * (c % 2) if kind == 1 else 3 - c
        bit = ((c + 1) // 2) % 2 if kind == 1 else c // 2
        return self.mesh_id(at, self.core), bit


def greet(place, others=()):
    barrier = pltpu.get_barrier_semaphore()
    partners = [place.sibling()] + [place.along(a, s)[0] for a in "xyz" for s in (1, 2, 3)] + list(others)
    for partner in partners:
        pl.semaphore_signal(barrier, inc=1, device_id=partner, device_id_type=pl.DeviceIdType.MESH)
    pl.semaphore_wait(barrier, len(partners))


class Sum:
    def __init__(self, place, u, g, done, got, send, recv):
        self.u, self.g, self.done, self.got, self.send, self.recv = u, g, done, got, send, recv
        self.stage, self.slots, self.copies = 0, 0, []
        order, first = ROUTES[u]
        self.steps, base, rows = [], 0, D

        def halve(name, target, bit, base, rows):
            rows //= 2
            self.steps.append((name, [(target, base + (1 - bit) * rows)], base + bit * rows, rows))
            return base + bit * rows, rows

        def quarter(name, axis, base, rows):
            rows //= 4
            peers = [place.along(axis, step) for step in (1, 2, 3)]
            self.steps.append((name, [(t, base + c * rows) for t, c in peers], base + place.at[axis] * rows, rows))
            return base + place.at[axis] * rows, rows

        base, rows = halve("core", place.sibling(), place.core, base, rows)
        if first:
            base, rows = halve("near", *place.across(order[0], first), base, rows)
            base, rows = halve("far", *place.across(order[0], 4 - first), base, rows)
        else:
            base, rows = quarter("axis", order[0], base, rows)
        base, rows = quarter("second", order[1], base, rows)
        peers = [place.along(order[2], step)[0] for step in (1, 2, 3)]
        self.swap = (peers, place.at[order[2]], base, rows)
        self.last = 2 * len(self.steps) + 1

    def part(self, ref, base, rows):
        return ref.at[self.u, pl.ds(pl.multiple_of(base, rows), rows), :]

    def copy(self, src, dst, target):
        slot = self.slots
        self.slots += 1
        one = pltpu.make_async_remote_copy(
            src_ref=src, dst_ref=dst, send_sem=self.send.at[self.u, slot], recv_sem=self.recv.at[self.u, slot],
            device_id=target, device_id_type=pl.DeviceIdType.MESH,
        )
        one.start()
        self.copies.append(one)

    def landing(self, name, i):
        if name == "axis":
            return self.got[name].at[i, self.u - QKV_BLOCKS[0]]
        return self.got[name].at[i, self.u]

    def advance(self):
        n, stage = len(self.steps), self.stage
        self.stage += 1
        for one in self.copies:
            one.wait()
        self.copies = []
        if 1 <= stage <= n:
            name, targets, base, rows = self.steps[stage - 1]
            mine = self.part(self.g, base, rows)
            total = mine[...].astype(F32)
            for i in range(len(targets)):
                total = total + self.landing(name, i)[...].astype(F32)
            mine[...] = total.astype(BF16)
        if stage == n + 1:
            _, _, base, rows = self.swap
            four = [self.got["swap"][c, self.u].astype(F32) for c in range(4)]
            self.part(self.done, base, rows)[...] = ((four[0] + four[1]) + (four[2] + four[3])).astype(BF16)
        if stage < n:
            name, targets, _, rows = self.steps[stage]
            for i, (target, base) in enumerate(targets):
                self.copy(self.part(self.g, base, rows), self.landing(name, i), target)
        elif stage == n:
            targets, at, base, rows = self.swap
            mine = self.part(self.g, base, rows)
            self.got["swap"][at, self.u] = mine[...]
            for target in targets:
                self.copy(mine, self.got["swap"].at[at, self.u], target)
        elif stage <= 2 * n:
            _, targets, base, rows = self.steps[2 * n - stage]
            mine = self.part(self.done, base, rows)
            for target, _ in targets:
                self.copy(mine, mine, target)


LANDINGS = (
    ("core", (1, BLOCKS, D // 2, D)),
    ("near", (1, BLOCKS - 3, D // 4, D)),
    ("far", (1, BLOCKS - 3, D // 8, D)),
    ("axis", (3, 3, D // 8, D)),
    ("second", (3, BLOCKS, D // 32, D)),
    ("swap", (4, BLOCKS, D // 32, D)),
)


def sum_scratch():
    return [pltpu.VMEM(shape, BF16) for _, shape in LANDINGS] + [pltpu.SemaphoreType.DMA((BLOCKS, SLOTS))] * 2


def unpack_kernel(g_ref, tok_ref, out_ref, in_ref, qkv_ref, proj_ref, tok_out, half, full, got, put, whole):
    def target(u):
        if u == PROJ_BLOCK:
            return proj_ref
        if u in OUT_BLOCKS:
            return out_ref.at[pl.ds(D * OUT_BLOCKS.index(u), D), :]
        if u in IN_BLOCKS:
            return in_ref.at[:, pl.ds(D * IN_BLOCKS.index(u), D)]
        return qkv_ref.at[:, pl.ds(D * QKV_BLOCKS.index(u), D)]

    ins = [pltpu.make_async_copy(g_ref.at[u], half.at[u], got.at[u]) for u in range(BLOCKS)]
    outs = [pltpu.make_async_copy(full.at[u], target(u), put.at[u]) for u in range(BLOCKS)]
    through = pltpu.make_async_copy(tok_ref, tok_out, whole)
    for one in ins:
        one.start()
    through.start()
    for u in range(BLOCKS):
        ins[u].wait()
        full[u] = half[u].astype(F32)
        outs[u].start()
    for one in outs:
        one.wait()
    through.wait()


def unpack_call(grads, grad_tokens):
    anywhere = pl.BlockSpec(memory_space=pl.ANY)
    return pl.pallas_call(
        unpack_kernel,
        out_shape=tuple(jax.ShapeDtypeStruct(s, F32) for s in ((FFN, D), (D, FFN), (D, 3 * D), (D, D), grad_tokens.shape)),
        in_specs=[anywhere] * 2,
        out_specs=(anywhere,) * 5,
        scratch_shapes=[
            pltpu.VMEM((BLOCKS, D, D), BF16),
            pltpu.VMEM((BLOCKS, D, D), F32),
            pltpu.SemaphoreType.DMA((BLOCKS,)),
            pltpu.SemaphoreType.DMA((BLOCKS,)),
            pltpu.SemaphoreType.DMA,
        ],
        compiler_params=pltpu.CompilerParams(vmem_limit_bytes=40 * 1024 * 1024),
        name="unpack",
    )(grads, grad_tokens)


LAT_ROWS, LON_ROWS = 32, 16
LAT_AT, LON_AT, DIAG_AT, HALO_ROWS = 0, 192, 336, 384
WINDOWS = 6
WIDE = 3
OWN_ROWS = 9
OWN_COLS = 30
HALO_PARTS = ((LAT_AT, LON_AT), (LON_AT, DIAG_AT), (DIAG_AT, HALO_ROWS))


def cell(level, row, wide, col=0):
    return ((row // WLAT) * WIDE + wide) * WIN + level * (WLAT * WLON) + (row % WLAT) * WLON + col


def padded(pieces, rows):
    have = sum(p.shape[0] for p in pieces)
    return jnp.concatenate(pieces + [jnp.zeros((rows - have, D), F32)], axis=0).astype(BF16)


def pack_ahead(src, dst):
    for level in range(WLEV):
        for row in range(HALF_LAT):
            at = LAT_AT + (level * HALF_LAT + row) * LAT_ROWS
            dst[at : at + LAT_ROWS, :] = padded([src[level, row, HALF_LON : HALF_LON + OWN_COLS, :]], LAT_ROWS)
    for row in range(HALF_LAT + OWN_ROWS):
        at = DIAG_AT + row * LON_ROWS if row < HALF_LAT else LON_AT + (row - HALF_LAT) * LON_ROWS
        dst[at : at + LON_ROWS, :] = padded([src[level, row, :HALF_LON, :] for level in range(WLEV)], LON_ROWS)


def place_strip(flat, level, row, strip):
    flat[cell(level, row, 0) : cell(level, row, 0) + WLON, :] = strip[:WLON]
    flat[cell(level, row, 1) : cell(level, row, 1) + WLON, :] = strip[WLON : 2 * WLON]
    flat[cell(level, row, 2) : cell(level, row, 2) + HALF_LON, :] = strip[2 * WLON : OWN_COLS]


def take_strip(flat, level, row):
    return [
        flat[cell(level, row, 0) : cell(level, row, 0) + WLON, :],
        flat[cell(level, row, 1) : cell(level, row, 1) + WLON, :],
        flat[cell(level, row, 2) : cell(level, row, 2) + HALF_LON, :],
    ]


def place_own(src, flat):
    for level in range(WLEV):
        for row in range(OWN_ROWS):
            place_strip(flat, level, row, src[level, row + HALF_LAT, HALF_LON : HALF_LON + OWN_COLS, :])


def place_halo(got, flat):
    for level in range(WLEV):
        for row in range(HALF_LAT):
            at = LAT_AT + (level * HALF_LAT + row) * LAT_ROWS
            place_strip(flat, level, OWN_ROWS + row, got[at : at + LAT_ROWS, :].astype(F32))
    for row in range(OWN_ROWS + HALF_LAT):
        at = LON_AT + row * LON_ROWS if row < OWN_ROWS else DIAG_AT + (row - OWN_ROWS) * LON_ROWS
        both = got[at : at + LON_ROWS, :].astype(F32)
        for level in range(WLEV):
            to = cell(level, row, 2, HALF_LON)
            flat[to : to + HALF_LON, :] = both[HALF_LON * level : HALF_LON * (level + 1)]


def pack_back(flat, dst):
    for level in range(WLEV):
        for row in range(HALF_LAT):
            at = LAT_AT + (level * HALF_LAT + row) * LAT_ROWS
            dst[at : at + LAT_ROWS, :] = padded(take_strip(flat, level, OWN_ROWS + row), LAT_ROWS)
    for row in range(OWN_ROWS + HALF_LAT):
        at = LON_AT + row * LON_ROWS if row < OWN_ROWS else DIAG_AT + (row - OWN_ROWS) * LON_ROWS
        ends = [cell(level, row, 2, HALF_LON) for level in range(WLEV)]
        dst[at : at + LON_ROWS, :] = padded([flat[e : e + HALF_LON, :] for e in ends], LON_ROWS)


def return_own(flat, out):
    for level in range(WLEV):
        for row in range(OWN_ROWS):
            out[level, row + HALF_LAT, HALF_LON : HALF_LON + OWN_COLS, :] = jnp.concatenate(
                take_strip(flat, level, row), axis=0
            )


def return_halo(got, out):
    for row in range(HALF_LAT + OWN_ROWS):
        at = DIAG_AT + row * LON_ROWS if row < HALF_LAT else LON_AT + (row - HALF_LAT) * LON_ROWS
        both = got[at : at + LON_ROWS, :].astype(F32)
        for level in range(WLEV):
            out[level, row, :HALF_LON, :] = both[HALF_LON * level : HALF_LON * (level + 1)]
    for level in range(WLEV):
        for row in range(HALF_LAT):
            at = LAT_AT + (level * HALF_LAT + row) * LAT_ROWS
            out[level, row, HALF_LON : HALF_LON + OWN_COLS, :] = got[at : at + LAT_ROWS, :].astype(F32)[:OWN_COLS]


AFTER_CHUNK = ((0, 1), (2, 3), (0, 1, 4, 5), (2, 3, 6, 7))
AFTER_PROJ = (8, 0, 1, 4, 5)
AFTER_WINDOW = ((2, 3, 6, 7), (8,), (0, 1, 4, 5), (2, 3, 6, 7), (8,), (0, 1, 4, 5))
AFTER_QKV = (2, 3, 6, 7, 8)
AFTER_INPUT = (0, 1, 4, 5)
AFTER_NORM = (9, 10, 11, 2, 3, 6, 7, 8)


def block_kernel(
    tokens, cotangent, region, wqkv, wproj, win, wout,
    out_ref, done_ref,
    cot_ref, x_ref, c_ref, wqkv_ref, wproj_ref, win_ref, wout_ref,
    normed, packed, probs, mixed, mid, nmid, dnm, g_ref,
    halo_out, halo_in, back_out, back_in, load_sem, halo_sem, *landings_and_sems,
):
    place = Place()
    *landings, send, recv = landings_and_sems
    got = {name: ref for (name, _), ref in zip(LANDINGS, landings)}
    sums = [Sum(place, u, g_ref, done_ref, got, send, recv) for u in range(BLOCKS)]

    def tick(*blocks):
        for u in blocks:
            sums[u].advance()

    loads = [
        pltpu.make_async_copy(src, dst, load_sem.at[i])
        for i, (src, dst) in enumerate(
            ((tokens, out_ref), (cotangent, cot_ref), (wqkv, wqkv_ref), (wproj, wproj_ref), (win, win_ref), (wout, wout_ref))
        )
    ]
    for one in loads:
        one.start()

    lat, lon = lax.axis_index("lat"), lax.axis_index("lon")
    lats, lons = lax.axis_size("lat"), lax.axis_size("lon")
    up, down = lax.rem(lat + lats - 1, lats), lax.rem(lat + 1, lats)
    left, right = lax.rem(lon + lons - 1, lons), lax.rem(lon + 1, lons)
    ahead = ((up, lon), (lat, left), (up, left))
    back = ((down, lon), (lat, right), (down, right))
    greet(place, ahead + back)

    def exchange(src, dst, targets, at):
        copies = []
        for i, (lo, hi) in enumerate(HALO_PARTS):
            one = pltpu.make_async_remote_copy(
                src_ref=src.at[lo:hi], dst_ref=dst.at[lo:hi],
                send_sem=halo_sem.at[0, at + i], recv_sem=halo_sem.at[1, at + i],
                device_id=targets[i], device_id_type=pl.DeviceIdType.MESH,
            )
            one.start()
            copies.append(one)
        return copies

    loads[0].wait()
    pack_ahead(out_ref, halo_out.at[0])
    token_halo = exchange(halo_out.at[0], halo_in.at[0], ahead, 0)
    loads[1].wait()
    pack_ahead(cot_ref, halo_out.at[1])
    cot_halo = exchange(halo_out.at[1], halo_in.at[1], ahead, 3)
    place_own(out_ref, x_ref)

    rows_of = lambda w: pl.ds(pl.multiple_of(w * WIN, WIN), WIN)

    def attention_forward(first, last):
        @pl.loop(first, last)
        def _(w):
            unit, _ = norm_parts(x_ref[rows_of(w), :])
            normed[rows_of(w), :] = unit.astype(BF16)

        if first == 0:
            loads[2].wait()
        rows = slice(first * WIN, last * WIN)
        for j in range(3):
            cols = slice(D * j, D * (j + 1))
            packed[rows, cols] = nn(normed[rows, :], wqkv_ref[:, cols]).astype(BF16)

        @pl.loop(first, last)
        def _(w):
            rows = rows_of(w)
            line = region[w]
            allowed = jnp.broadcast_to(line, (WIN, WIN)).T[:, :1] == jnp.concatenate([line] * GROUP, axis=1)
            for g in range(GROUPS):
                lo = LANES * g
                q = packed[rows, lo : lo + LANES]
                k = packed[rows, D + lo : D + lo + LANES]
                v = packed[rows, 2 * D + lo : 2 * D + lo + LANES]
                s = jnp.where(allowed, nt(k, spread_heads(q)), MASKED)
                e = jnp.exp2((s - jnp.max(s, axis=0, keepdims=True)) * (SCALE * LOG2E))
                p = (e * (1.0 / jnp.sum(e, axis=0, keepdims=True))).astype(BF16)
                probs[w * GROUPS + g] = p
                mixed[rows, lo : lo + LANES] = own_blocks(nn(v.T, p)).T.astype(BF16)

    attention_forward(0, 2)
    for one in token_halo:
        one.wait()
    place_halo(halo_in.at[0], x_ref)
    attention_forward(2, WINDOWS)

    loads[3].wait()
    mid[...] = nn(mixed[...], wproj_ref[...]).astype(BF16).astype(F32)

    @pl.loop(0, WINDOWS)
    def _(w):
        rows = rows_of(w)
        middle = x_ref[rows, :] + mid[rows, :]
        mid[rows, :] = middle
        nmid[rows, :] = norm_parts(middle)[0].astype(BF16)

    place_own(cot_ref, c_ref)
    for one in cot_halo:
        one.wait()
    place_halo(halo_in.at[1], c_ref)
    loads[4].wait()
    loads[5].wait()

    nmid_t = nmid[...].T
    for j in range(FFN // D):
        cols = slice(D * j, D * (j + 1))
        cot = c_ref[...].astype(BF16)
        u = nn(nmid[...], win_ref[:, cols])
        da = nt(cot, wout_ref[cols, :])
        square = u * u
        t = jnp.tanh(u * (GELU_A + (GELU_A * GELU_B) * square))
        half = 0.5 + 0.5 * t
        act = (u * half).astype(BF16)
        slope = half + u * (0.5 - 0.5 * t * t) * (GELU_A + (3 * GELU_A * GELU_B) * square)
        dpre = (slope * da).astype(BF16)
        g_ref[OUT_BLOCKS[j]] = nn(act.T, cot).astype(BF16)
        g_ref[IN_BLOCKS[j]] = nn(nmid_t, dpre).astype(BF16)
        part = nt(dpre, win_ref[:, cols])
        if j == 0:
            dnm[...] = part
        else:
            dnm[...] += part
        tick(*AFTER_CHUNK[j])

    @pl.loop(0, WINDOWS)
    def _(w):
        rows = rows_of(w)
        unit, r = norm_parts(mid[rows, :])
        d_mid = c_ref[rows, :] + norm_back(unit, r, dnm[rows, :])
        c_ref[rows, :] = d_mid
        nmid[rows, :] = d_mid.astype(BF16)

    g_ref[PROJ_BLOCK] = nn(mixed[...].T, nmid[...]).astype(BF16)
    tick(*AFTER_PROJ)
    mixed[...] = nt(nmid[...], wproj_ref[...]).astype(BF16)

    for w in range(WINDOWS):

        @pl.loop(w, w + 1)
        def _(w):
            rows = rows_of(w)
            for g in range(GROUPS):
                lo = LANES * g
                q = spread_heads(packed[rows, lo : lo + LANES])
                k = packed[rows, D + lo : D + lo + LANES]
                v = packed[rows, 2 * D + lo : 2 * D + lo + LANES]
                do = spread_heads(mixed[rows, lo : lo + LANES])
                p = probs[w * GROUPS + g]
                dp = nt(v, do)
                pf = p.astype(F32)
                total = jnp.sum(dp * pf, axis=0, keepdims=True)
                ds = (pf * (dp - total) * SCALE).astype(BF16)
                packed[rows, lo : lo + LANES] = own_blocks(nn(k.T, ds)).T.astype(BF16)
                packed[rows, D + lo : D + lo + LANES] = nn(ds, q).astype(BF16)
                packed[rows, 2 * D + lo : 2 * D + lo + LANES] = nn(p, do).astype(BF16)

        tick(*AFTER_WINDOW[w])

    normed_t = normed[...].T
    for j in range(3):
        g_ref[QKV_BLOCKS[j]] = nn(normed_t, packed[:, D * j : D * (j + 1)]).astype(BF16)
        tick(QKV_BLOCKS[j])
    tick(*AFTER_QKV)
    for j in range(3):
        cols = slice(D * j, D * (j + 1))
        part = nt(packed[:, cols], wqkv_ref[:, cols])
        if j == 0:
            dnm[...] = part
        else:
            dnm[...] += part
    tick(*AFTER_INPUT)

    @pl.loop(0, WINDOWS)
    def _(w):
        rows = rows_of(w)
        unit, r = norm_parts(x_ref[rows, :])
        c_ref[rows, :] = c_ref[rows, :] + norm_back(unit, r, dnm[rows, :])

    tick(*AFTER_NORM)
    pack_back(c_ref, back_out)
    grad_halo = exchange(back_out, back_in, back, 6)
    return_own(c_ref, out_ref)

    rounds = 0
    while any(one.stage <= one.last for one in sums):
        tick(*(u for u in (9, 10, 11, 0, 1, 2, 3, 4, 5, 6, 7, 8) if sums[u].stage <= sums[u].last))
        rounds += 1
        if rounds == 2:
            for one in grad_halo:
                one.wait()
            return_halo(back_in, out_ref)


def block_call(tokens, cotangent, region, w_qkv, w_proj, w_in, w_out):
    anywhere, vmem = pl.BlockSpec(memory_space=pl.ANY), pl.BlockSpec(memory_space=pltpu.VMEM)
    cells = WINDOWS * WIN
    return pl.pallas_call(
        block_kernel,
        out_shape=(jax.ShapeDtypeStruct(tokens.shape, F32), jax.ShapeDtypeStruct((BLOCKS, D, D), BF16)),
        in_specs=[anywhere, anywhere, vmem] + [anywhere] * 4,
        out_specs=(vmem, vmem),
        scratch_shapes=[
            pltpu.VMEM(tokens.shape, F32),
            pltpu.VMEM((cells, D), F32),
            pltpu.VMEM((cells, D), F32),
            pltpu.VMEM(w_qkv.shape, BF16),
            pltpu.VMEM(w_proj.shape, BF16),
            pltpu.VMEM(w_in.shape, BF16),
            pltpu.VMEM(w_out.shape, BF16),
            pltpu.VMEM((cells, D), BF16),
            pltpu.VMEM((cells, 3 * D), BF16),
            pltpu.VMEM((WINDOWS * GROUPS, WIN, SPREAD), BF16),
            pltpu.VMEM((cells, D), BF16),
            pltpu.VMEM((cells, D), F32),
            pltpu.VMEM((cells, D), BF16),
            pltpu.VMEM((cells, D), F32),
            pltpu.VMEM((BLOCKS, D, D), BF16),
            pltpu.VMEM((2, HALO_ROWS, D), BF16),
            pltpu.VMEM((2, HALO_ROWS, D), BF16),
            pltpu.VMEM((HALO_ROWS, D), BF16),
            pltpu.VMEM((HALO_ROWS, D), BF16),
            pltpu.SemaphoreType.DMA((6,)),
            pltpu.SemaphoreType.DMA((2, 9)),
        ]
        + sum_scratch(),
        compiler_params=pltpu.CompilerParams(
            collective_id=0, has_side_effects=True, vmem_limit_bytes=63 * 1024 * 1024
        ),
        cost_estimate=pl.CostEstimate(flops=16 * 10**9, bytes_accessed=24 * 10**6, transcendentals=4 * 10**6),
        name="block",
    )(tokens, cotangent, region, w_qkv, w_proj, w_in, w_out)


def local(tokens, cotangent, region_ids, w_qkv, w_proj, w_in, w_out):
    levels, rows_lat, cols_lon = region_ids.shape
    region = region_ids[::-1].reshape(levels, rows_lat // WLAT, WLAT, cols_lon // WLON, WLON)
    region = region.transpose(1, 3, 0, 2, 4).reshape(-1, 1, WIN).astype(F32)
    grad_tokens, grads = block_call(tokens, cotangent, region, w_qkv, w_proj, w_in, w_out)
    grad_out, grad_in, grad_qkv, grad_proj, grad_tokens = unpack_call(grads, grad_tokens)
    return grad_tokens, grad_qkv, grad_proj, grad_in, grad_out


def solution(mesh):
    grid = P(None, "lat", "lon", None)
    in_specs = (grid, grid, P(None, "lat", "lon"), P(), P(), P(), P())
    out_specs = (grid, P(), P(), P(), P())
    return jax.shard_map(local, mesh=mesh, in_specs=in_specs, out_specs=out_specs, check_vma=False)
```

time: 441 us -> 119 us (0.27); the launches traced: 435 us -> 119 us
  waiting for transfers between devices: 145 us -> 0 us
  matrix products: 117 us -> 0 us
  Pallas kernels: 0 us -> 105 us
  local copies, waits for them, and re-layouts: 118 us -> 13.2 us
  other arithmetic: 23.8 us -> 0.01 us
  starting transfers between devices: 16.3 us -> 0 us
  between operations: 15.1 us -> 0.68 us
    psum x1 -> x0, waiting for transfers between devices: 120 us -> none  [local(): lax.psum((grad_qkv, grad_proj, grad_in, grad_out), ('lat', 'lon'))]
    pallas_call x0 -> x2, Pallas kernels: none -> 105 us  [the longest x1 99.2 us: block_call(): pl.pallas_call(block_kernel, out_shape=(jax.ShapeDtypeStruct(tokens.shape...]
    dot_general x16 -> x0, matrix products: 104 us -> none  [the longest x1 20.5 us: core_backward(): jnp.einsum('whqk,wqhd->wkhd', d_scores, queries, preferred_element_type=j...]
    convert_element_type x9 -> x3, local copies, waits for them, and re-layouts: 56.5 us -> 0.8 us  [local(): region = region.transpose(1, 3, 0, 2, 4).reshape(-1, 1, WIN).astype(F32)]
    ppermute x8 -> x0, waiting for transfers between devices: 25.7 us -> none  [passed_along(): return lax.ppermute(value, axis, pairs)]
    ppermute x8 -> x0, starting transfers between devices: 16.3 us -> none  [passed_along(): return lax.ppermute(value, axis, pairs)]
    reduce_sum x7 -> x0, other arithmetic: 13.2 us -> none  [the longest x4 7.52 us: norm_rows(): centred = values - jnp.mean(values, axis=-1, keepdims=True)]
    sub x1 -> x0, matrix products: 12.9 us -> none  [core_forward(): soft = jax.nn.softmax(scores, axis=-1)]
  transfers between devices with their start and end apart: 9 -> 0, of which waited for: 7 -> 0; matrix products, arithmetic and copies ran while one was open for 13% -> 0% of each run, Pallas kernels for 0% -> 0%
where the time goes in v1:
time: 119 us
  Pallas kernels  105 us (88%)
  local copies, waits for them, and re-layouts  13.2 us (11%)
    pallas_call x1, Pallas kernels, block_call(): pl.pallas_call(block_kernel, out_shape=(jax.ShapeDtypeStruct(tokens.shape...  99.2 us
    unnamed x9, local copies, waits for them, and re-layouts  11.6 us
    pallas_call x1, Pallas kernels, unpack_call(): pl.pallas_call(unpack_kernel, out_shape=tuple((jax.ShapeDtypeStruct(s, F3...  5.57 us

profile of v1, /device:TPU:1, one launch (start us, length us, event | category | flops | bytes accessed | tf_op | source)
XLA Modules:
  0.0 118.6 jit_solution(5191578651370692870)
XLA Ops:
  0.6 0.7 rev.3
  1.4 0.0 copy-start.2
  1.4 0.1 convert_element_type.10
  1.5 0.7 convert_element_type.13.region
  2.2 3.1 %copy.17.tokens = f32[2,12,36,512]{3,2,1,0:T(8,128)} copy(f32[2,12,36,512]{3,0,2,1:T(2,128)} %param.7) | data formatting | bytes 3538944 | tf_op args[0]
  5.3 0.0 copy-done.2
  5.3 1.6 %copy.18.cotangent = f32[2,12,36,512]{3,2,1,0:T(8,128)} copy(f32[2,12,36,512]{3,0,2,1:T(2,128)S(1)} %copy-done.2) | data formatting | bytes 3538944 | tf_op args[1]
  6.9 99.2 %block.1 = (f32[2,12,36,512]{3,2,1,0:T(8,128)}, bf16[12,512,512]{2,1,0:T(8,128)(2,1)}) custom-call(f32[2,12,36,512]{3,2,1,0:T(8,128)} %copy.17.tokens, f32[2,12,36,512]{3,2,1,0:T(8,128)} %copy.18.cotangent, f32[6,1,144]{2,1,0:T(1,128)} %convert_element_type.13.region, bf16[512,1536]{1,0:T(8,128)(2,1)} %wqkv.1, bf16[512,512]{1,0:T(8,128)(2,1)} %wproj.1, ...), custom_call_target="tpu_custom_call" | custom-call | flops 16000000000 | bytes 24000000 | tf_op jit(solution)/shard_map/block/pallas_call | solution.py:548
  106.1 0.0 copy-start
  106.1 2.8 %copy-done = bf16[12,512,512]{2,1,0:T(8,128)(2,1)S(1)} copy-done((bf16[12,512,512]{2,1,0:T(8,128)(2,1)S(1)}, bf16[12,512,512]{2,1,0:T(8,128)(2,1)}, u32[]{:S(2)}) %copy-start) | copy-done | bytes 6291480
  108.9 0.0 copy-start.1
  108.9 1.5 %copy-done.1 = f32[2,12,36,512]{3,2,1,0:T(8,128)S(1)} copy-done((f32[2,12,36,512]{3,2,1,0:T(8,128)S(1)}, f32[2,12,36,512]{3,2,1,0:T(8,128)}, u32[]{:S(2)}) %copy-start.1) | copy-done | bytes 1769496
  110.5 5.6 %unpack.1 = (f32[2048,512]{1,0:T(8,128)}, f32[512,2048]{1,0:T(8,128)}, f32[512,1536]{1,0:T(8,128)}, f32[512,512]{1,0:T(8,128)}, f32[2,12,36,512]{3,2,1,0:T(8,128)S(1)}) custom-call(bf16[12,512,512]{2,1,0:T(8,128)(2,1)S(1)} %copy-done, f32[2,12,36,512]{3,2,1,0:T(8,128)S(1)} %copy-done.1), custom_call_target="tpu_custom_call" | custom-call | tf_op jit(solution)/shard_map/unpack/pallas_call | solution.py:231
  116.0 2.6 %copy.20 = f32[2,12,36,512]{3,0,2,1:T(2,128)} copy(f32[2,12,36,512]{3,2,1,0:T(8,128)S(1)} %get-tuple-element.24) | data formatting | bytes 3538944
  (2 shorter events, 0.0 us)
Async XLA Ops:
  1.4 3.9 %copy-start.2 = (f32[2,12,36,512]{3,0,2,1:T(2,128)S(1)}, f32[2,12,36,512]{3,0,2,1:T(2,128)}, u32[]{:S(2)}) copy-start(f32[2,12,36,512]{3,0,2,1:T(2,128)} %param.8) | copy-start | bytes 5308420
  106.1 2.8 %copy-start = (bf16[12,512,512]{2,1,0:T(8,128)(2,1)S(1)}, bf16[12,512,512]{2,1,0:T(8,128)(2,1)}, u32[]{:S(2)}) copy-start(bf16[12,512,512]{2,1,0:T(8,128)(2,1)} %get-tuple-element.12.g_ref) | copy-start | bytes 18874372
  108.9 1.5 %copy-start.1 = (f32[2,12,36,512]{3,2,1,0:T(8,128)S(1)}, f32[2,12,36,512]{3,2,1,0:T(8,128)}, u32[]{:S(2)}) copy-start(f32[2,12,36,512]{3,2,1,0:T(8,128)} %get-tuple-element.13.tok_ref) | copy-start | bytes 5308420

commit v2 on v1

--- a/solution.py
+++ b/solution.py
@@ -201,7 +201,7 @@
     return [pltpu.VMEM(shape, BF16) for _, shape in LANDINGS] + [pltpu.SemaphoreType.DMA((BLOCKS, SLOTS))] * 2
 
 
-def unpack_kernel(g_ref, tok_ref, out_ref, in_ref, qkv_ref, proj_ref, tok_out, half, full, got, put, whole):
+def unpack_kernel(g_ref, tok_ref, out_ref, in_ref, qkv_ref, proj_ref, tok_out, half, full, lines_in, got, put, whole):
     def target(u):
         if u == PROJ_BLOCK:
             return proj_ref
@@ -213,17 +213,20 @@
 
     ins = [pltpu.make_async_copy(g_ref.at[u], half.at[u], got.at[u]) for u in range(BLOCKS)]
     outs = [pltpu.make_async_copy(full.at[u], target(u), put.at[u]) for u in range(BLOCKS)]
-    through = pltpu.make_async_copy(tok_ref, tok_out, whole)
+    arrive = pltpu.make_async_copy(tok_ref, lines_in, whole.at[0])
+    leave = pltpu.make_async_copy(lines_in, tok_out, whole.at[1])
+    arrive.start()
     for one in ins:
         one.start()
-    through.start()
+    arrive.wait()
+    leave.start()
     for u in range(BLOCKS):
         ins[u].wait()
         full[u] = half[u].astype(F32)
         outs[u].start()
     for one in outs:
         one.wait()
-    through.wait()
+    leave.wait()
 
 
 def unpack_call(grads, grad_tokens):
@@ -236,26 +239,41 @@
         scratch_shapes=[
             pltpu.VMEM((BLOCKS, D, D), BF16),
             pltpu.VMEM((BLOCKS, D, D), F32),
+            pltpu.VMEM(grad_tokens.shape, F32),
             pltpu.SemaphoreType.DMA((BLOCKS,)),
             pltpu.SemaphoreType.DMA((BLOCKS,)),
-            pltpu.SemaphoreType.DMA,
+            pltpu.SemaphoreType.DMA((2,)),
         ],
-        compiler_params=pltpu.CompilerParams(vmem_limit_bytes=40 * 1024 * 1024),
+        compiler_params=pltpu.CompilerParams(vmem_limit_bytes=60 * 1024 * 1024),
         name="unpack",
     )(grads, grad_tokens)
 
 
-LAT_ROWS, LON_ROWS = 32, 16
+LAT_ROWS, LON_ROWS = 64, 16
 LAT_AT, LON_AT, DIAG_AT, HALO_ROWS = 0, 192, 336, 384
 WINDOWS = 6
+FEW = 48
+TINY = 16
+PIECE = 256
 WIDE = 3
 OWN_ROWS = 9
 OWN_COLS = 30
+STRIP = OWN_COLS * WLEV
+EDGE = HALF_LON * WLEV
+LINE = WLON * WLEV
 HALO_PARTS = ((LAT_AT, LON_AT), (LON_AT, DIAG_AT), (DIAG_AT, HALO_ROWS))
 
 
-def cell(level, row, wide, col=0):
-    return ((row // WLAT) * WIDE + wide) * WIN + level * (WLAT * WLON) + (row % WLAT) * WLON + col
+def cell(row, wide):
+    return ((row // WLAT) * WIDE + wide) * WIN + (row % WLAT) * LINE
+
+
+def lines(v):
+    return v.reshape(v.shape[0] * WLEV, D)
+
+
+def cells(v):
+    return v.reshape(v.shape[0] // WLEV, WLEV, D)
 
 
 def padded(pieces, rows):
@@ -263,103 +281,112 @@
     return jnp.concatenate(pieces + [jnp.zeros((rows - have, D), F32)], axis=0).astype(BF16)
 
 
+def ahead_at(row):
+    return DIAG_AT + row * LON_ROWS if row < HALF_LAT else LON_AT + (row - HALF_LAT) * LON_ROWS
+
+
+def behind_at(row):
+    return LON_AT + row * LON_ROWS if row < OWN_ROWS else DIAG_AT + (row - OWN_ROWS) * LON_ROWS
+
+
 def pack_ahead(src, dst):
-    for level in range(WLEV):
-        for row in range(HALF_LAT):
-            at = LAT_AT + (level * HALF_LAT + row) * LAT_ROWS
-            dst[at : at + LAT_ROWS, :] = padded([src[level, row, HALF_LON : HALF_LON + OWN_COLS, :]], LAT_ROWS)
+    for row in range(HALF_LAT):
+        at = LAT_AT + row * LAT_ROWS
+        dst[at : at + LAT_ROWS, :] = padded([lines(src[row, HALF_LON : HALF_LON + OWN_COLS])], LAT_ROWS)
     for row in range(HALF_LAT + OWN_ROWS):
-        at = DIAG_AT + row * LON_ROWS if row < HALF_LAT else LON_AT + (row - HALF_LAT) * LON_ROWS
-        dst[at : at + LON_ROWS, :] = padded([src[level, row, :HALF_LON, :] for level in range(WLEV)], LON_ROWS)
-
-
-def place_strip(flat, level, row, strip):
-    flat[cell(level, row, 0) : cell(level, row, 0) + WLON, :] = strip[:WLON]
-    flat[cell(level, row, 1) : cell(level, row, 1) + WLON, :] = strip[WLON : 2 * WLON]
-    flat[cell(level, row, 2) : cell(level, row, 2) + HALF_LON, :] = strip[2 * WLON : OWN_COLS]
-
-
-def take_strip(flat, level, row):
+        at = ahead_at(row)
+        dst[at : at + LON_ROWS, :] = padded([lines(src[row, :HALF_LON])], LON_ROWS)
+
+
+def place_strip(flat, row, strip):
+    flat[cell(row, 0) : cell(row, 0) + LINE, :] = strip[:LINE]
+    flat[cell(row, 1) : cell(row, 1) + LINE, :] = strip[LINE : 2 * LINE]
+    flat[cell(row, 2) : cell(row, 2) + EDGE, :] = strip[2 * LINE : STRIP]
+
+
+def take_strip(flat, row):
     return [
-        flat[cell(level, row, 0) : cell(level, row, 0) + WLON, :],
-        flat[cell(level, row, 1) : cell(level, row, 1) + WLON, :],
-        flat[cell(level, row, 2) : cell(level, row, 2) + HALF_LON, :],
+        flat[cell(row, 0) : cell(row, 0) + LINE, :],
+        flat[cell(row, 1) : cell(row, 1) + LINE, :],
+        flat[cell(row, 2) : cell(row, 2) + EDGE, :],
     ]
 
 
 def place_own(src, flat):
-    for level in range(WLEV):
-        for row in range(OWN_ROWS):
-            place_strip(flat, level, row, src[level, row + HALF_LAT, HALF_LON : HALF_LON + OWN_COLS, :])
+    for row in range(OWN_ROWS):
+        place_strip(flat, row, lines(src[row + HALF_LAT, HALF_LON : HALF_LON + OWN_COLS]))
 
 
 def place_halo(got, flat):
-    for level in range(WLEV):
-        for row in range(HALF_LAT):
-            at = LAT_AT + (level * HALF_LAT + row) * LAT_ROWS
-            place_strip(flat, level, OWN_ROWS + row, got[at : at + LAT_ROWS, :].astype(F32))
+    for row in range(HALF_LAT):
+        at = LAT_AT + row * LAT_ROWS
+        place_strip(flat, OWN_ROWS + row, got[at : at + LAT_ROWS, :].astype(F32))
     for row in range(OWN_ROWS + HALF_LAT):
-        at = LON_AT + row * LON_ROWS if row < OWN_ROWS else DIAG_AT + (row - OWN_ROWS) * LON_ROWS
-        both = got[at : at + LON_ROWS, :].astype(F32)
-        for level in range(WLEV):
-            to = cell(level, row, 2, HALF_LON)
-            flat[to : to + HALF_LON, :] = both[HALF_LON * level : HALF_LON * (level + 1)]
+        at, to = behind_at(row), cell(row, 2) + EDGE
+        flat[to : to + EDGE, :] = got[at : at + LON_ROWS, :].astype(F32)[:EDGE]
 
 
 def pack_back(flat, dst):
-    for level in range(WLEV):
-        for row in range(HALF_LAT):
-            at = LAT_AT + (level * HALF_LAT + row) * LAT_ROWS
-            dst[at : at + LAT_ROWS, :] = padded(take_strip(flat, level, OWN_ROWS + row), LAT_ROWS)
+    for row in range(HALF_LAT):
+        at = LAT_AT + row * LAT_ROWS
+        dst[at : at + LAT_ROWS, :] = padded(take_strip(flat, OWN_ROWS + row), LAT_ROWS)
     for row in range(OWN_ROWS + HALF_LAT):
-        at = LON_AT + row * LON_ROWS if row < OWN_ROWS else DIAG_AT + (row - OWN_ROWS) * LON_ROWS
-        ends = [cell(level, row, 2, HALF_LON) for level in range(WLEV)]
-        dst[at : at + LON_ROWS, :] = padded([flat[e : e + HALF_LON, :] for e in ends], LON_ROWS)
+        at, end = behind_at(row), cell(row, 2) + EDGE
+        dst[at : at + LON_ROWS, :] = padded([flat[end : end + EDGE, :]], LON_ROWS)
 
 
 def return_own(flat, out):
-    for level in range(WLEV):
-        for row in range(OWN_ROWS):
-            out[level, row + HALF_LAT, HALF_LON : HALF_LON + OWN_COLS, :] = jnp.concatenate(
-                take_strip(flat, level, row), axis=0
-            )
+    for row in range(OWN_ROWS):
+        strip = jnp.concatenate(take_strip(flat, row), axis=0)
+        out[row + HALF_LAT, HALF_LON : HALF_LON + OWN_COLS] = cells(strip)
 
 
 def return_halo(got, out):
     for row in range(HALF_LAT + OWN_ROWS):
-        at = DIAG_AT + row * LON_ROWS if row < HALF_LAT else LON_AT + (row - HALF_LAT) * LON_ROWS
-        both = got[at : at + LON_ROWS, :].astype(F32)
-        for level in range(WLEV):
-            out[level, row, :HALF_LON, :] = both[HALF_LON * level : HALF_LON * (level + 1)]
-    for level in range(WLEV):
-        for row in range(HALF_LAT):
-            at = LAT_AT + (level * HALF_LAT + row) * LAT_ROWS
-            out[level, row, HALF_LON : HALF_LON + OWN_COLS, :] = got[at : at + LAT_ROWS, :].astype(F32)[:OWN_COLS]
-
-
-AFTER_CHUNK = ((0, 1), (2, 3), (0, 1, 4, 5), (2, 3, 6, 7))
-AFTER_PROJ = (8, 0, 1, 4, 5)
-AFTER_WINDOW = ((2, 3, 6, 7), (8,), (0, 1, 4, 5), (2, 3, 6, 7), (8,), (0, 1, 4, 5))
-AFTER_QKV = (2, 3, 6, 7, 8)
-AFTER_INPUT = (0, 1, 4, 5)
-AFTER_NORM = (9, 10, 11, 2, 3, 6, 7, 8)
+        at = ahead_at(row)
+        out[row, :HALF_LON] = cells(got[at : at + LON_ROWS, :].astype(F32)[:EDGE])
+    for row in range(HALF_LAT):
+        at = LAT_AT + row * LAT_ROWS
+        out[row, HALF_LON : HALF_LON + OWN_COLS] = cells(got[at : at + LAT_ROWS, :].astype(F32)[:STRIP])
+
+
+def place_regions(region, flat):
+    for row in range(HALF_LAT + OWN_ROWS):
+        ids = region[row].astype(F32)
+        levels = [jnp.broadcast_to(ids[l : l + 1], (128, ids.shape[1])).T for l in range(WLEV)]
+        both = jnp.stack(levels[::-1], axis=1).reshape(ids.shape[1] * WLEV, 128)
+        for wide in range(WIDE):
+            flat[cell(row, wide) : cell(row, wide) + LINE, :] = both[LINE * wide : LINE * (wide + 1)]
+
+
+AFTER_CHUNK = ((0, 1), (0, 1, 2, 3), (2, 3, 4, 5), (0, 1, 4, 5, 6, 7))
+AFTER_PROJ = (8, 2, 3, 6, 7)
+AFTER_WINDOW = ((0, 1, 8), (4, 5), (2, 3), (0, 1, 6, 7), (4, 5, 8), (2, 3))
+AFTER_QKV = (0, 1, 6, 7, 8)
+AFTER_INPUT = (9, 10, 11, 4, 5)
+AFTER_NORM = (0, 1, 2, 3, 6, 7, 8)
 
 
 def block_kernel(
     tokens, cotangent, region, wqkv, wproj, win, wout,
-    out_ref, done_ref,
-    cot_ref, x_ref, c_ref, wqkv_ref, wproj_ref, win_ref, wout_ref,
+    out_ref, done_hbm,
+    done_ref, cot_ref, region_ref, x_ref, c_ref, wqkv_ref, wproj_ref, win_ref, wout_ref,
     normed, packed, probs, mixed, mid, nmid, dnm, g_ref,
-    halo_out, halo_in, back_out, back_in, load_sem, halo_sem, *landings_and_sems,
+    pre, dact, act, dpre, cot_half, dscores,
+    halo_out, halo_in, back_out, back_in, load_sem, halo_sem, done_sem, *landings_and_sems,
 ):
     place = Place()
     *landings, send, recv = landings_and_sems
     got = {name: ref for (name, _), ref in zip(LANDINGS, landings)}
     sums = [Sum(place, u, g_ref, done_ref, got, send, recv) for u in range(BLOCKS)]
 
+    leaving = {u: pltpu.make_async_copy(done_ref.at[u], done_hbm.at[u], done_sem.at[u]) for u in range(BLOCKS)}
+
     def tick(*blocks):
         for u in blocks:
             sums[u].advance()
+            if sums[u].stage == sums[u].last + 1:
+                leaving[u].start()
 
     loads = [
         pltpu.make_async_copy(src, dst, load_sem.at[i])
@@ -397,14 +424,18 @@
     pack_ahead(cot_ref, halo_out.at[1])
     cot_halo = exchange(halo_out.at[1], halo_in.at[1], ahead, 3)
     place_own(out_ref, x_ref)
+    place_regions(region, region_ref)
 
     rows_of = lambda w: pl.ds(pl.multiple_of(w * WIN, WIN), WIN)
+    few_of = lambda i: pl.ds(pl.multiple_of(i * FEW, FEW), FEW)
+    fews = WIN // FEW
+    pieces = [(c, min(c + PIECE, SPREAD)) for c in range(0, SPREAD, PIECE)]
 
     def attention_forward(first, last):
-        @pl.loop(first, last)
-        def _(w):
-            unit, _ = norm_parts(x_ref[rows_of(w), :])
-            normed[rows_of(w), :] = unit.astype(BF16)
+        @pl.loop(first * fews, last * fews)
+        def _(i):
+            unit, _ = norm_parts(x_ref[few_of(i), :])
+            normed[few_of(i), :] = unit.astype(BF16)
 
         if first == 0:
             loads[2].wait()
@@ -416,18 +447,20 @@
         @pl.loop(first, last)
         def _(w):
             rows = rows_of(w)
-            line = region[w]
-            allowed = jnp.broadcast_to(line, (WIN, WIN)).T[:, :1] == jnp.concatenate([line] * GROUP, axis=1)
+            ids = region_ref[rows, :]
+            of_key, of_query = ids[:, :1], jnp.concatenate([ids.T[:1]] * GROUP, axis=1)
             for g in range(GROUPS):
                 lo = LANES * g
                 q = packed[rows, lo : lo + LANES]
                 k = packed[rows, D + lo : D + lo + LANES]
                 v = packed[rows, 2 * D + lo : 2 * D + lo + LANES]
-                s = jnp.where(allowed, nt(k, spread_heads(q)), MASKED)
-                e = jnp.exp2((s - jnp.max(s, axis=0, keepdims=True)) * (SCALE * LOG2E))
-                p = (e * (1.0 / jnp.sum(e, axis=0, keepdims=True))).astype(BF16)
-                probs[w * GROUPS + g] = p
-                mixed[rows, lo : lo + LANES] = own_blocks(nn(v.T, p)).T.astype(BF16)
+                q = spread_heads(q)
+                for c0, c1 in pieces:
+                    s = jnp.where(of_key == of_query[:, c0:c1], nt(k, q[c0:c1]), MASKED)
+                    e = jnp.exp2((s - jnp.max(s, axis=0, keepdims=True)) * (SCALE * LOG2E))
+                    p = e * (1.0 / jnp.sum(e, axis=0, keepdims=True))
+                    probs[w * GROUPS + g, :, c0:c1] = p.astype(BF16)
+                mixed[rows, lo : lo + LANES] = own_blocks(nn(v.T, probs[w * GROUPS + g])).T.astype(BF16)
 
     attention_forward(0, 2)
     for one in token_halo:
@@ -438,9 +471,9 @@
     loads[3].wait()
     mid[...] = nn(mixed[...], wproj_ref[...]).astype(BF16).astype(F32)
 
-    @pl.loop(0, WINDOWS)
-    def _(w):
-        rows = rows_of(w)
+    @pl.loop(0, WINDOWS * fews)
+    def _(i):
+        rows = few_of(i)
         middle = x_ref[rows, :] + mid[rows, :]
         mid[rows, :] = middle
         nmid[rows, :] = norm_parts(middle)[0].astype(BF16)
@@ -453,29 +486,35 @@
     loads[5].wait()
 
     nmid_t = nmid[...].T
+    cot_half[...] = c_ref[...].astype(BF16)
     for j in range(FFN // D):
         cols = slice(D * j, D * (j + 1))
-        cot = c_ref[...].astype(BF16)
-        u = nn(nmid[...], win_ref[:, cols])
-        da = nt(cot, wout_ref[cols, :])
-        square = u * u
-        t = jnp.tanh(u * (GELU_A + (GELU_A * GELU_B) * square))
-        half = 0.5 + 0.5 * t
-        act = (u * half).astype(BF16)
-        slope = half + u * (0.5 - 0.5 * t * t) * (GELU_A + (3 * GELU_A * GELU_B) * square)
-        dpre = (slope * da).astype(BF16)
-        g_ref[OUT_BLOCKS[j]] = nn(act.T, cot).astype(BF16)
-        g_ref[IN_BLOCKS[j]] = nn(nmid_t, dpre).astype(BF16)
-        part = nt(dpre, win_ref[:, cols])
+        pre[...] = nn(nmid[...], win_ref[:, cols])
+        dact[...] = nt(cot_half[...], wout_ref[cols, :])
+
+        @pl.loop(0, WINDOWS * WIN // TINY, unroll=2)
+        def _(i):
+            rows = pl.ds(pl.multiple_of(i * TINY, TINY), TINY)
+            u = pre[rows, :]
+            square = u * u
+            t = jnp.tanh(u * (GELU_A + (GELU_A * GELU_B) * square))
+            half = 0.5 + 0.5 * t
+            act[rows, :] = (u * half).astype(BF16)
+            slope = half + u * (0.5 - 0.5 * t * t) * (GELU_A + (3 * GELU_A * GELU_B) * square)
+            dpre[rows, :] = (slope * dact[rows, :]).astype(BF16)
+
+        g_ref[OUT_BLOCKS[j]] = nn(act[...].T, cot_half[...]).astype(BF16)
+        g_ref[IN_BLOCKS[j]] = nn(nmid_t, dpre[...]).astype(BF16)
+        part = nt(dpre[...], win_ref[:, cols])
         if j == 0:
             dnm[...] = part
         else:
             dnm[...] += part
         tick(*AFTER_CHUNK[j])
 
-    @pl.loop(0, WINDOWS)
-    def _(w):
-        rows = rows_of(w)
+    @pl.loop(0, WINDOWS * fews)
+    def _(i):
+        rows = few_of(i)
         unit, r = norm_parts(mid[rows, :])
         d_mid = c_ref[rows, :] + norm_back(unit, r, dnm[rows, :])
         c_ref[rows, :] = d_mid
@@ -497,10 +536,12 @@
                 v = packed[rows, 2 * D + lo : 2 * D + lo + LANES]
                 do = spread_heads(mixed[rows, lo : lo + LANES])
                 p = probs[w * GROUPS + g]
-                dp = nt(v, do)
-                pf = p.astype(F32)
-                total = jnp.sum(dp * pf, axis=0, keepdims=True)
-                ds = (pf * (dp - total) * SCALE).astype(BF16)
+                for c0, c1 in pieces:
+                    dp = nt(v, do[c0:c1])
+                    pf = probs[w * GROUPS + g, :, c0:c1].astype(F32)
+                    total = jnp.sum(dp * pf, axis=0, keepdims=True)
+                    dscores[:, c0:c1] = (pf * (dp - total) * SCALE).astype(BF16)
+                ds = dscores[...]
                 packed[rows, lo : lo + LANES] = own_blocks(nn(k.T, ds)).T.astype(BF16)
                 packed[rows, D + lo : D + lo + LANES] = nn(ds, q).astype(BF16)
                 packed[rows, 2 * D + lo : 2 * D + lo + LANES] = nn(p, do).astype(BF16)
@@ -521,9 +562,9 @@
             dnm[...] += part
     tick(*AFTER_INPUT)
 
-    @pl.loop(0, WINDOWS)
-    def _(w):
-        rows = rows_of(w)
+    @pl.loop(0, WINDOWS * fews)
+    def _(i):
+        rows = few_of(i)
         unit, r = norm_parts(x_ref[rows, :])
         c_ref[rows, :] = c_ref[rows, :] + norm_back(unit, r, dnm[rows, :])
 
@@ -540,38 +581,49 @@
             for one in grad_halo:
                 one.wait()
             return_halo(back_in, out_ref)
+    for one in leaving.values():
+        one.wait()
 
 
 def block_call(tokens, cotangent, region, w_qkv, w_proj, w_in, w_out):
     anywhere, vmem = pl.BlockSpec(memory_space=pl.ANY), pl.BlockSpec(memory_space=pltpu.VMEM)
-    cells = WINDOWS * WIN
+    count = WINDOWS * WIN
     return pl.pallas_call(
         block_kernel,
         out_shape=(jax.ShapeDtypeStruct(tokens.shape, F32), jax.ShapeDtypeStruct((BLOCKS, D, D), BF16)),
         in_specs=[anywhere, anywhere, vmem] + [anywhere] * 4,
-        out_specs=(vmem, vmem),
+        out_specs=(vmem, anywhere),
         scratch_shapes=[
+            pltpu.VMEM((BLOCKS, D, D), BF16),
             pltpu.VMEM(tokens.shape, F32),
-            pltpu.VMEM((cells, D), F32),
-            pltpu.VMEM((cells, D), F32),
+            pltpu.VMEM((count, 128), F32),
+            pltpu.VMEM((count, D), F32),
+            pltpu.VMEM((count, D), F32),
             pltpu.VMEM(w_qkv.shape, BF16),
             pltpu.VMEM(w_proj.shape, BF16),
             pltpu.VMEM(w_in.shape, BF16),
             pltpu.VMEM(w_out.shape, BF16),
-            pltpu.VMEM((cells, D), BF16),
-            pltpu.VMEM((cells, 3 * D), BF16),
+            pltpu.VMEM((count, D), BF16),
+            pltpu.VMEM((count, 3 * D), BF16),
             pltpu.VMEM((WINDOWS * GROUPS, WIN, SPREAD), BF16),
-            pltpu.VMEM((cells, D), BF16),
-            pltpu.VMEM((cells, D), F32),
-            pltpu.VMEM((cells, D), BF16),
-            pltpu.VMEM((cells, D), F32),
+            pltpu.VMEM((count, D), BF16),
+            pltpu.VMEM((count, D), F32),
+            pltpu.VMEM((count, D), BF16),
+            pltpu.VMEM((count, D), F32),
             pltpu.VMEM((BLOCKS, D, D), BF16),
+            pltpu.VMEM((count, D), F32),
+            pltpu.VMEM((count, D), F32),
+            pltpu.VMEM((count, D), BF16),
+            pltpu.VMEM((count, D), BF16),
+            pltpu.VMEM((count, D), BF16),
+            pltpu.VMEM((WIN, SPREAD), BF16),
             pltpu.VMEM((2, HALO_ROWS, D), BF16),
             pltpu.VMEM((2, HALO_ROWS, D), BF16),
             pltpu.VMEM((HALO_ROWS, D), BF16),
             pltpu.VMEM((HALO_ROWS, D), BF16),
             pltpu.SemaphoreType.DMA((6,)),
             pltpu.SemaphoreType.DMA((2, 9)),
+            pltpu.SemaphoreType.DMA((BLOCKS,)),
         ]
         + sum_scratch(),
         compiler_params=pltpu.CompilerParams(
@@ -583,12 +635,12 @@
 
 
 def local(tokens, cotangent, region_ids, w_qkv, w_proj, w_in, w_out):
-    levels, rows_lat, cols_lon = region_ids.shape
-    region = region_ids[::-1].reshape(levels, rows_lat // WLAT, WLAT, cols_lon // WLON, WLON)
-    region = region.transpose(1, 3, 0, 2, 4).reshape(-1, 1, WIN).astype(F32)
-    grad_tokens, grads = block_call(tokens, cotangent, region, w_qkv, w_proj, w_in, w_out)
+    grad_tokens, grads = block_call(
+        tokens.transpose(1, 2, 0, 3), cotangent.transpose(1, 2, 0, 3), region_ids.transpose(1, 0, 2),
+        w_qkv, w_proj, w_in, w_out,
+    )
     grad_out, grad_in, grad_qkv, grad_proj, grad_tokens = unpack_call(grads, grad_tokens)
-    return grad_tokens, grad_qkv, grad_proj, grad_in, grad_out
+    return grad_tokens.transpose(2, 0, 1, 3), grad_qkv, grad_proj, grad_in, grad_out
 
 
 def solution(mesh):

time: 119 us -> 118 us (level)
  local copies, waits for them, and re-layouts: 13.2 us -> 0 us
  Pallas kernels: 105 us -> 117 us
    unnamed x9 -> x0, local copies, waits for them, and re-layouts: 11.6 us -> none
    pallas_call x1, Pallas kernels: 99.2 us -> 108 us  [block_call(): pl.pallas_call(block_kernel, out_shape=(jax.ShapeDtypeStruct(tokens.shape...]
    pallas_call x1, Pallas kernels: 5.57 us -> 8.57 us  [unpack_call(): pl.pallas_call(unpack_kernel, out_shape=tuple((jax.ShapeDtypeStruct(s, F3...]
where the time goes in v2:
time: 118 us
  Pallas kernels  117 us (99%)
    pallas_call x1, Pallas kernels, block_call(): pl.pallas_call(block_kernel, out_shape=(jax.ShapeDtypeStruct(tokens.shape...  108 us
    pallas_call x1, Pallas kernels, unpack_call(): pl.pallas_call(unpack_kernel, out_shape=tuple((jax.ShapeDtypeStruct(s, F3...  8.57 us

profile of v2, /device:TPU:1, one launch (start us, length us, event | category | flops | bytes accessed | tf_op | source)
XLA Modules:
  0.0 117.8 jit_solution(10928951229364007167)
XLA Ops:
  0.6 108.4 %block.1 = (f32[12,36,2,512]{3,2,1,0:T(2,128)}, bf16[12,512,512]{2,1,0:T(8,128)(2,1)}) custom-call(f32[12,36,2,512]{3,2,1,0:T(2,128)} %bitcast.4, f32[12,36,2,512]{3,2,1,0:T(2,128)} %bitcast.5, s32[12,2,36]{2,1,0:T(2,128)} %bitcast.7, bf16[512,1536]{1,0:T(8,128)(2,1)} %wqkv.1, bf16[512,512]{1,0:T(8,128)(2,1)} %wproj.1, bf16[512,2048]{1,0:T(8,128)(2,1)} %win.1, ...), custom_call_target="tpu_custom_call" | custom-call | flops 16000000000 | bytes 24000000 | tf_op jit(solution)/shard_map/block/pallas_call | solution.py:591
  109.1 8.6 %unpack.1 = (f32[2048,512]{1,0:T(8,128)}, f32[512,2048]{1,0:T(8,128)}, f32[512,1536]{1,0:T(8,128)}, f32[512,512]{1,0:T(8,128)}, f32[12,36,2,512]{3,2,1,0:T(2,128)}) custom-call(bf16[12,512,512]{2,1,0:T(8,128)(2,1)} %get-tuple-element.12.g_ref, f32[12,36,2,512]{3,2,1,0:T(2,128)} %get-tuple-element.13.tok_ref), custom_call_target="tpu_custom_call" | custom-call | tf_op jit(solution)/shard_map/unpack/pallas_call | solution.py:234

commit v3 on v2

--- a/solution.py
+++ b/solution.py
@@ -252,7 +252,7 @@
 LAT_ROWS, LON_ROWS = 64, 16
 LAT_AT, LON_AT, DIAG_AT, HALO_ROWS = 0, 192, 336, 384
 WINDOWS = 6
-FEW = 48
+FEW = 144
 TINY = 16
 PIECE = 256
 WIDE = 3
@@ -359,12 +359,12 @@
             flat[cell(row, wide) : cell(row, wide) + LINE, :] = both[LINE * wide : LINE * (wide + 1)]
 
 
-AFTER_CHUNK = ((0, 1), (0, 1, 2, 3), (2, 3, 4, 5), (0, 1, 4, 5, 6, 7))
-AFTER_PROJ = (8, 2, 3, 6, 7)
-AFTER_WINDOW = ((0, 1, 8), (4, 5), (2, 3), (0, 1, 6, 7), (4, 5, 8), (2, 3))
-AFTER_QKV = (0, 1, 6, 7, 8)
-AFTER_INPUT = (9, 10, 11, 4, 5)
-AFTER_NORM = (0, 1, 2, 3, 6, 7, 8)
+AFTER_CHUNK = ((0, 1), (2, 3), (0, 1, 4, 5), (2, 3, 6, 7))
+AFTER_PROJ = (8, 0, 1, 4, 5)
+AFTER_WINDOW = ((2, 3, 6, 7), (8,), (0, 1, 4, 5), (2, 3, 6, 7), (8,), (0, 1, 4, 5))
+AFTER_QKV = (2, 3, 6, 7, 8)
+AFTER_INPUT = (9, 10, 11, 0, 1, 4, 5)
+AFTER_NORM = (2, 3, 6, 7, 8)
 
 
 def block_kernel(
@@ -492,7 +492,7 @@
         pre[...] = nn(nmid[...], win_ref[:, cols])
         dact[...] = nt(cot_half[...], wout_ref[cols, :])
 
-        @pl.loop(0, WINDOWS * WIN // TINY, unroll=2)
+        @pl.loop(0, WINDOWS * WIN // TINY, unroll=9)
         def _(i):
             rows = pl.ds(pl.multiple_of(i * TINY, TINY), TINY)
             u = pre[rows, :]

time: 118 us -> 109 us (0.924)
  Pallas kernels: 117 us -> 109 us
    pallas_call x1, Pallas kernels: 108 us -> 99.9 us  [block_call(): pl.pallas_call(block_kernel, out_shape=(jax.ShapeDtypeStruct(tokens.shape...]
where the time goes in v3:
time: 109 us
  Pallas kernels  109 us (100%)
    pallas_call x1, Pallas kernels, block_call(): pl.pallas_call(block_kernel, out_shape=(jax.ShapeDtypeStruct(tokens.shape...  99.9 us
    pallas_call x1, Pallas kernels, unpack_call(): pl.pallas_call(unpack_kernel, out_shape=tuple((jax.ShapeDtypeStruct(s, F3...  8.57 us

profile of v3, /device:TPU:1, one launch (start us, length us, event | category | flops | bytes accessed | tf_op | source)
XLA Modules:
  0.0 109.3 jit_solution(2385552301669323452)
XLA Ops:
  0.6 99.9 %block.1 = (f32[12,36,2,512]{3,2,1,0:T(2,128)}, bf16[12,512,512]{2,1,0:T(8,128)(2,1)}) custom-call(f32[12,36,2,512]{3,2,1,0:T(2,128)} %bitcast.4, f32[12,36,2,512]{3,2,1,0:T(2,128)} %bitcast.5, s32[12,2,36]{2,1,0:T(2,128)} %bitcast.7, bf16[512,1536]{1,0:T(8,128)(2,1)} %wqkv.1, bf16[512,512]{1,0:T(8,128)(2,1)} %wproj.1, bf16[512,2048]{1,0:T(8,128)(2,1)} %win.1, ...), custom_call_target="tpu_custom_call" | custom-call | flops 16000000000 | bytes 24000000 | tf_op jit(solution)/shard_map/block/pallas_call | solution.py:591
  100.6 8.6 %unpack.1 = (f32[2048,512]{1,0:T(8,128)}, f32[512,2048]{1,0:T(8,128)}, f32[512,1536]{1,0:T(8,128)}, f32[512,512]{1,0:T(8,128)}, f32[12,36,2,512]{3,2,1,0:T(2,128)}) custom-call(bf16[12,512,512]{2,1,0:T(8,128)(2,1)} %get-tuple-element.12.g_ref, f32[12,36,2,512]{3,2,1,0:T(2,128)} %get-tuple-element.13.tok_ref), custom_call_target="tpu_custom_call" | custom-call | tf_op jit(solution)/shard_map/unpack/pallas_call | solution.py:234

commit v4 on v3

--- a/solution.py
+++ b/solution.py
@@ -66,11 +66,11 @@
 IN_BLOCKS = (1, 3, 5, 7)
 PROJ_BLOCK = 8
 QKV_BLOCKS = (9, 10, 11)
-ROUTES = (
-    ("xyz", 1), ("yzx", 1), ("zxy", 1), ("xyz", 3), ("yzx", 3), ("zxy", 3),
-    ("xyz", 1), ("yzx", 1), ("zxy", 1),
-    ("xyz", 0), ("yzx", 0), ("zxy", 0),
+UNITS = (
+    (0, 2, "xyz", 1), (2, 2, "yzx", 1), (4, 2, "zxy", 1), (6, 2, "xyz", 3),
+    (8, 1, "yzx", 0), (9, 1, "xyz", 0), (10, 1, "yzx", 0), (11, 1, "zxy", 0),
 )
+DIRECT = 8
 SLOTS = 17
 
 
@@ -108,9 +108,10 @@
 
 class Sum:
     def __init__(self, place, u, g, done, got, send, recv):
+        self.first, self.count, order, first = UNITS[u]
+        self.blocks = pl.ds(self.first, self.count)
         self.u, self.g, self.done, self.got, self.send, self.recv = u, g, done, got, send, recv
         self.stage, self.slots, self.copies = 0, 0, []
-        order, first = ROUTES[u]
         self.steps, base, rows = [], 0, D
 
         def halve(name, target, bit, base, rows):
@@ -136,7 +137,7 @@
         self.last = 2 * len(self.steps) + 1
 
     def part(self, ref, base, rows):
-        return ref.at[self.u, pl.ds(pl.multiple_of(base, rows), rows), :]
+        return ref.at[self.blocks, pl.ds(pl.multiple_of(base, rows), rows), :]
 
     def copy(self, src, dst, target):
         slot = self.slots
@@ -150,8 +151,8 @@
 
     def landing(self, name, i):
         if name == "axis":
-            return self.got[name].at[i, self.u - QKV_BLOCKS[0]]
-        return self.got[name].at[i, self.u]
+            return self.got[name].at[i, pl.ds(self.first - DIRECT, self.count)]
+        return self.got[name].at[i, self.blocks]
 
     def advance(self):
         n, stage = len(self.steps), self.stage
@@ -168,7 +169,7 @@
             mine[...] = total.astype(BF16)
         if stage == n + 1:
             _, _, base, rows = self.swap
-            four = [self.got["swap"][c, self.u].astype(F32) for c in range(4)]
+            four = [self.got["swap"][c, self.blocks].astype(F32) for c in range(4)]
             self.part(self.done, base, rows)[...] = ((four[0] + four[1]) + (four[2] + four[3])).astype(BF16)
         if stage < n:
             name, targets, _, rows = self.steps[stage]
@@ -177,9 +178,9 @@
         elif stage == n:
             targets, at, base, rows = self.swap
             mine = self.part(self.g, base, rows)
-            self.got["swap"][at, self.u] = mine[...]
+            self.got["swap"][at, self.blocks] = mine[...]
             for target in targets:
-                self.copy(mine, self.got["swap"].at[at, self.u], target)
+                self.copy(mine, self.got["swap"].at[at, self.blocks], target)
         elif stage <= 2 * n:
             _, targets, base, rows = self.steps[2 * n - stage]
             mine = self.part(self.done, base, rows)
@@ -189,16 +190,16 @@
 
 LANDINGS = (
     ("core", (1, BLOCKS, D // 2, D)),
-    ("near", (1, BLOCKS - 3, D // 4, D)),
-    ("far", (1, BLOCKS - 3, D // 8, D)),
-    ("axis", (3, 3, D // 8, D)),
+    ("near", (1, DIRECT, D // 4, D)),
+    ("far", (1, DIRECT, D // 8, D)),
+    ("axis", (3, BLOCKS - DIRECT, D // 8, D)),
     ("second", (3, BLOCKS, D // 32, D)),
     ("swap", (4, BLOCKS, D // 32, D)),
 )
 
 
 def sum_scratch():
-    return [pltpu.VMEM(shape, BF16) for _, shape in LANDINGS] + [pltpu.SemaphoreType.DMA((BLOCKS, SLOTS))] * 2
+    return [pltpu.VMEM(shape, BF16) for _, shape in LANDINGS] + [pltpu.SemaphoreType.DMA((len(UNITS), SLOTS))] * 2
 
 
 def unpack_kernel(g_ref, tok_ref, out_ref, in_ref, qkv_ref, proj_ref, tok_out, half, full, lines_in, got, put, whole):
@@ -359,12 +360,13 @@
             flat[cell(row, wide) : cell(row, wide) + LINE, :] = both[LINE * wide : LINE * (wide + 1)]
 
 
-AFTER_CHUNK = ((0, 1), (2, 3), (0, 1, 4, 5), (2, 3, 6, 7))
-AFTER_PROJ = (8, 0, 1, 4, 5)
-AFTER_WINDOW = ((2, 3, 6, 7), (8,), (0, 1, 4, 5), (2, 3, 6, 7), (8,), (0, 1, 4, 5))
-AFTER_QKV = (2, 3, 6, 7, 8)
-AFTER_INPUT = (9, 10, 11, 0, 1, 4, 5)
-AFTER_NORM = (2, 3, 6, 7, 8)
+QKV_UNITS = (5, 6, 7)
+AFTER_CHUNK = ((0,), (0, 1), (1, 2), (0, 2, 3))
+AFTER_PROJ = (4, 0, 1, 3)
+AFTER_WINDOW = ((), (0, 1, 2, 4), (3,), (0, 1, 2), (4,), (0, 1, 2, 3))
+AFTER_QKV = (4,)
+AFTER_INPUT = (5, 6, 7, 0, 1, 2, 3)
+AFTER_NORM = (4,)
 
 
 def block_kernel(
@@ -378,9 +380,11 @@
     place = Place()
     *landings, send, recv = landings_and_sems
     got = {name: ref for (name, _), ref in zip(LANDINGS, landings)}
-    sums = [Sum(place, u, g_ref, done_ref, got, send, recv) for u in range(BLOCKS)]
-
-    leaving = {u: pltpu.make_async_copy(done_ref.at[u], done_hbm.at[u], done_sem.at[u]) for u in range(BLOCKS)}
+    sums = [Sum(place, u, g_ref, done_ref, got, send, recv) for u in range(len(UNITS))]
+
+    leaving = [
+        pltpu.make_async_copy(done_ref.at[one.blocks], done_hbm.at[one.blocks], done_sem.at[one.u]) for one in sums
+    ]
 
     def tick(*blocks):
         for u in blocks:
@@ -551,7 +555,7 @@
     normed_t = normed[...].T
     for j in range(3):
         g_ref[QKV_BLOCKS[j]] = nn(normed_t, packed[:, D * j : D * (j + 1)]).astype(BF16)
-        tick(QKV_BLOCKS[j])
+        tick(QKV_UNITS[j])
     tick(*AFTER_QKV)
     for j in range(3):
         cols = slice(D * j, D * (j + 1))
@@ -575,13 +579,13 @@
 
     rounds = 0
     while any(one.stage <= one.last for one in sums):
-        tick(*(u for u in (9, 10, 11, 0, 1, 2, 3, 4, 5, 6, 7, 8) if sums[u].stage <= sums[u].last))
+        tick(*(u for u in (*QKV_UNITS, 0, 1, 2, 3, 4) if sums[u].stage <= sums[u].last))
         rounds += 1
         if rounds == 2:
             for one in grad_halo:
                 one.wait()
             return_halo(back_in, out_ref)
-    for one in leaving.values():
+    for one in leaving:
         one.wait()
 
 
@@ -623,7 +627,7 @@
             pltpu.VMEM((HALO_ROWS, D), BF16),
             pltpu.SemaphoreType.DMA((6,)),
             pltpu.SemaphoreType.DMA((2, 9)),
-            pltpu.SemaphoreType.DMA((BLOCKS,)),
+            pltpu.SemaphoreType.DMA((len(UNITS),)),
         ]
         + sum_scratch(),
         compiler_params=pltpu.CompilerParams(

time: 109 us -> 119 us (1.092)
  Pallas kernels: 109 us -> 118 us
    pallas_call x1, Pallas kernels: 99.9 us -> 109 us  [block_call(): pl.pallas_call(block_kernel, out_shape=(jax.ShapeDtypeStruct(tokens.shape...]
where the time goes in v4:
time: 119 us
  Pallas kernels  118 us (99%)
    pallas_call x1, Pallas kernels, block_call(): pl.pallas_call(block_kernel, out_shape=(jax.ShapeDtypeStruct(tokens.shape...  109 us
    pallas_call x1, Pallas kernels, unpack_call(): pl.pallas_call(unpack_kernel, out_shape=tuple((jax.ShapeDtypeStruct(s, F3...  8.57 us

profile of v4, /device:TPU:1, one launch (start us, length us, event | category | flops | bytes accessed | tf_op | source)
XLA Modules:
  0.0 118.8 jit_solution(2098562018854572263)
XLA Ops:
  0.6 109.5 %block.1 = (f32[12,36,2,512]{3,2,1,0:T(2,128)}, bf16[12,512,512]{2,1,0:T(8,128)(2,1)}) custom-call(f32[12,36,2,512]{3,2,1,0:T(2,128)} %bitcast.4, f32[12,36,2,512]{3,2,1,0:T(2,128)} %bitcast.5, s32[12,2,36]{2,1,0:T(2,128)} %bitcast.7, bf16[512,1536]{1,0:T(8,128)(2,1)} %wqkv.1, bf16[512,512]{1,0:T(8,128)(2,1)} %wproj.1, bf16[512,2048]{1,0:T(8,128)(2,1)} %win.1, ...), custom_call_target="tpu_custom_call" | custom-call | flops 16000000000 | bytes 24000000 | tf_op jit(solution)/shard_map/block/pallas_call | solution.py:595
  110.1 8.6 %unpack.1 = (f32[2048,512]{1,0:T(8,128)}, f32[512,2048]{1,0:T(8,128)}, f32[512,1536]{1,0:T(8,128)}, f32[512,512]{1,0:T(8,128)}, f32[12,36,2,512]{3,2,1,0:T(2,128)}) custom-call(bf16[12,512,512]{2,1,0:T(8,128)(2,1)} %get-tuple-element.12.g_ref, f32[12,36,2,512]{3,2,1,0:T(2,128)} %get-tuple-element.13.tok_ref), custom_call_target="tpu_custom_call" | custom-call | tf_op jit(solution)/shard_map/unpack/pallas_call | solution.py:235

commit v5 on v3

--- a/solution.py
+++ b/solution.py
@@ -68,7 +68,7 @@
 QKV_BLOCKS = (9, 10, 11)
 ROUTES = (
     ("xyz", 1), ("yzx", 1), ("zxy", 1), ("xyz", 3), ("yzx", 3), ("zxy", 3),
-    ("xyz", 1), ("yzx", 1), ("zxy", 1),
+    ("xyz", 1), ("yzx", 1), ("zxy", 0),
     ("xyz", 0), ("yzx", 0), ("zxy", 0),
 )
 SLOTS = 17
@@ -150,7 +150,7 @@
 
     def landing(self, name, i):
         if name == "axis":
-            return self.got[name].at[i, self.u - QKV_BLOCKS[0]]
+            return self.got[name].at[i, self.u - PROJ_BLOCK]
         return self.got[name].at[i, self.u]
 
     def advance(self):
@@ -191,7 +191,7 @@
     ("core", (1, BLOCKS, D // 2, D)),
     ("near", (1, BLOCKS - 3, D // 4, D)),
     ("far", (1, BLOCKS - 3, D // 8, D)),
-    ("axis", (3, 3, D // 8, D)),
+    ("axis", (3, 4, D // 8, D)),
     ("second", (3, BLOCKS, D // 32, D)),
     ("swap", (4, BLOCKS, D // 32, D)),
 )
@@ -253,8 +253,6 @@
 LAT_AT, LON_AT, DIAG_AT, HALO_ROWS = 0, 192, 336, 384
 WINDOWS = 6
 FEW = 144
-TINY = 16
-PIECE = 256
 WIDE = 3
 OWN_ROWS = 9
 OWN_COLS = 30
@@ -359,12 +357,12 @@
             flat[cell(row, wide) : cell(row, wide) + LINE, :] = both[LINE * wide : LINE * (wide + 1)]
 
 
-AFTER_CHUNK = ((0, 1), (2, 3), (0, 1, 4, 5), (2, 3, 6, 7))
-AFTER_PROJ = (8, 0, 1, 4, 5)
-AFTER_WINDOW = ((2, 3, 6, 7), (8,), (0, 1, 4, 5), (2, 3, 6, 7), (8,), (0, 1, 4, 5))
-AFTER_QKV = (2, 3, 6, 7, 8)
-AFTER_INPUT = (9, 10, 11, 0, 1, 4, 5)
-AFTER_NORM = (2, 3, 6, 7, 8)
+AFTER_CHUNK = ((0, 1), (0, 1, 2, 3), (2, 3, 4, 5), (0, 1, 4, 5, 6, 7))
+AFTER_PROJ = (8, 0, 1, 2, 3, 6, 7)
+AFTER_WINDOW = ((4, 5), (0, 1, 2, 3, 8), (4, 5, 6, 7), (0, 1, 2, 3), (4, 5, 6, 7, 8), (0, 1, 2, 3))
+AFTER_QKV = (4, 5, 6, 7, 8)
+AFTER_INPUT = (9, 10, 11, 0, 1, 2, 3)
+AFTER_NORM = (4, 5, 6, 7, 8)
 
 
 def block_kernel(
@@ -372,7 +370,6 @@
     out_ref, done_hbm,
     done_ref, cot_ref, region_ref, x_ref, c_ref, wqkv_ref, wproj_ref, win_ref, wout_ref,
     normed, packed, probs, mixed, mid, nmid, dnm, g_ref,
-    pre, dact, act, dpre, cot_half, dscores,
     halo_out, halo_in, back_out, back_in, load_sem, halo_sem, done_sem, *landings_and_sems,
 ):
     place = Place()
@@ -420,16 +417,12 @@
     loads[0].wait()
     pack_ahead(out_ref, halo_out.at[0])
     token_halo = exchange(halo_out.at[0], halo_in.at[0], ahead, 0)
-    loads[1].wait()
-    pack_ahead(cot_ref, halo_out.at[1])
-    cot_halo = exchange(halo_out.at[1], halo_in.at[1], ahead, 3)
     place_own(out_ref, x_ref)
     place_regions(region, region_ref)
 
     rows_of = lambda w: pl.ds(pl.multiple_of(w * WIN, WIN), WIN)
     few_of = lambda i: pl.ds(pl.multiple_of(i * FEW, FEW), FEW)
     fews = WIN // FEW
-    pieces = [(c, min(c + PIECE, SPREAD)) for c in range(0, SPREAD, PIECE)]
 
     def attention_forward(first, last):
         @pl.loop(first * fews, last * fews)
@@ -448,23 +441,24 @@
         def _(w):
             rows = rows_of(w)
             ids = region_ref[rows, :]
-            of_key, of_query = ids[:, :1], jnp.concatenate([ids.T[:1]] * GROUP, axis=1)
+            allowed = ids[:, :1] == jnp.concatenate([ids.T[:1]] * GROUP, axis=1)
             for g in range(GROUPS):
                 lo = LANES * g
                 q = packed[rows, lo : lo + LANES]
                 k = packed[rows, D + lo : D + lo + LANES]
                 v = packed[rows, 2 * D + lo : 2 * D + lo + LANES]
-                q = spread_heads(q)
-                for c0, c1 in pieces:
-                    s = jnp.where(of_key == of_query[:, c0:c1], nt(k, q[c0:c1]), MASKED)
-                    e = jnp.exp2((s - jnp.max(s, axis=0, keepdims=True)) * (SCALE * LOG2E))
-                    p = e * (1.0 / jnp.sum(e, axis=0, keepdims=True))
-                    probs[w * GROUPS + g, :, c0:c1] = p.astype(BF16)
-                mixed[rows, lo : lo + LANES] = own_blocks(nn(v.T, probs[w * GROUPS + g])).T.astype(BF16)
+                s = jnp.where(allowed, nt(k, spread_heads(q)), MASKED)
+                e = jnp.exp2((s - jnp.max(s, axis=0, keepdims=True)) * (SCALE * LOG2E))
+                p = (e * (1.0 / jnp.sum(e, axis=0, keepdims=True))).astype(BF16)
+                probs[w * GROUPS + g] = p
+                mixed[rows, lo : lo + LANES] = own_blocks(nn(v.T, p)).T.astype(BF16)
 
     attention_forward(0, 2)
+    loads[1].wait()
+    pack_ahead(cot_ref, halo_out.at[1])
     for one in token_halo:
         one.wait()
+    cot_halo = exchange(halo_out.at[1], halo_in.at[1], ahead, 3)
     place_halo(halo_in.at[0], x_ref)
     attention_forward(2, WINDOWS)
 
@@ -486,26 +480,20 @@
     loads[5].wait()
 
     nmid_t = nmid[...].T
-    cot_half[...] = c_ref[...].astype(BF16)
     for j in range(FFN // D):
         cols = slice(D * j, D * (j + 1))
-        pre[...] = nn(nmid[...], win_ref[:, cols])
-        dact[...] = nt(cot_half[...], wout_ref[cols, :])
-
-        @pl.loop(0, WINDOWS * WIN // TINY, unroll=9)
-        def _(i):
-            rows = pl.ds(pl.multiple_of(i * TINY, TINY), TINY)
-            u = pre[rows, :]
-            square = u * u
-            t = jnp.tanh(u * (GELU_A + (GELU_A * GELU_B) * square))
-            half = 0.5 + 0.5 * t
-            act[rows, :] = (u * half).astype(BF16)
-            slope = half + u * (0.5 - 0.5 * t * t) * (GELU_A + (3 * GELU_A * GELU_B) * square)
-            dpre[rows, :] = (slope * dact[rows, :]).astype(BF16)
-
-        g_ref[OUT_BLOCKS[j]] = nn(act[...].T, cot_half[...]).astype(BF16)
-        g_ref[IN_BLOCKS[j]] = nn(nmid_t, dpre[...]).astype(BF16)
-        part = nt(dpre[...], win_ref[:, cols])
+        cot = c_ref[...].astype(BF16)
+        u = nn(nmid[...], win_ref[:, cols])
+        da = nt(cot, wout_ref[cols, :])
+        square = u * u
+        t = jnp.tanh(u * (GELU_A + (GELU_A * GELU_B) * square))
+        half = 0.5 + 0.5 * t
+        act = (u * half).astype(BF16)
+        slope = half + u * (0.5 - 0.5 * t * t) * (GELU_A + (3 * GELU_A * GELU_B) * square)
+        dpre = (slope * da).astype(BF16)
+        g_ref[OUT_BLOCKS[j]] = nn(act.T, cot).astype(BF16)
+        g_ref[IN_BLOCKS[j]] = nn(nmid_t, dpre).astype(BF16)
+        part = nt(dpre, win_ref[:, cols])
         if j == 0:
             dnm[...] = part
         else:
@@ -536,12 +524,10 @@
                 v = packed[rows, 2 * D + lo : 2 * D + lo + LANES]
                 do = spread_heads(mixed[rows, lo : lo + LANES])
                 p = probs[w * GROUPS + g]
-                for c0, c1 in pieces:
-                    dp = nt(v, do[c0:c1])
-                    pf = probs[w * GROUPS + g, :, c0:c1].astype(F32)
-                    total = jnp.sum(dp * pf, axis=0, keepdims=True)
-                    dscores[:, c0:c1] = (pf * (dp - total) * SCALE).astype(BF16)
-                ds = dscores[...]
+                dp = nt(v, do)
+                pf = p.astype(F32)
+                total = jnp.sum(dp * pf, axis=0, keepdims=True)
+                ds = (pf * (dp - total) * SCALE).astype(BF16)
                 packed[rows, lo : lo + LANES] = own_blocks(nn(k.T, ds)).T.astype(BF16)
                 packed[rows, D + lo : D + lo + LANES] = nn(ds, q).astype(BF16)
                 packed[rows, 2 * D + lo : 2 * D + lo + LANES] = nn(p, do).astype(BF16)
@@ -611,12 +597,6 @@
             pltpu.VMEM((count, D), BF16),
             pltpu.VMEM((count, D), F32),
             pltpu.VMEM((BLOCKS, D, D), BF16),
-            pltpu.VMEM((count, D), F32),
-            pltpu.VMEM((count, D), F32),
-            pltpu.VMEM((count, D), BF16),
-            pltpu.VMEM((count, D), BF16),
-            pltpu.VMEM((count, D), BF16),
-            pltpu.VMEM((WIN, SPREAD), BF16),
             pltpu.VMEM((2, HALO_ROWS, D), BF16),
             pltpu.VMEM((2, HALO_ROWS, D), BF16),
             pltpu.VMEM((HALO_ROWS, D), BF16),

time: 109 us -> 110 us (level)
  no operation moved by 1% of the time
where the time goes in v5:
time: 110 us
  Pallas kernels  109 us (99%)
    pallas_call x1, Pallas kernels, block_call(): pl.pallas_call(block_kernel, out_shape=(jax.ShapeDtypeStruct(tokens.shape...  101 us
    pallas_call x1, Pallas kernels, unpack_call(): pl.pallas_call(unpack_kernel, out_shape=tuple((jax.ShapeDtypeStruct(s, F3...  8.57 us

profile of v5, /device:TPU:1, one launch (start us, length us, event | category | flops | bytes accessed | tf_op | source)
XLA Modules:
  0.0 110.1 jit_solution(17875013461367511736)
XLA Ops:
  0.6 100.7 %block.1 = (f32[12,36,2,512]{3,2,1,0:T(2,128)}, bf16[12,512,512]{2,1,0:T(8,128)(2,1)}) custom-call(f32[12,36,2,512]{3,2,1,0:T(2,128)} %bitcast.4, f32[12,36,2,512]{3,2,1,0:T(2,128)} %bitcast.5, s32[12,2,36]{2,1,0:T(2,128)} %bitcast.7, bf16[512,1536]{1,0:T(8,128)(2,1)} %wqkv.1, bf16[512,512]{1,0:T(8,128)(2,1)} %wproj.1, bf16[512,2048]{1,0:T(8,128)(2,1)} %win.1, ...), custom_call_target="tpu_custom_call" | custom-call | flops 16000000000 | bytes 24000000 | tf_op jit(solution)/shard_map/block/pallas_call | solution.py:577
  101.3 8.6 %unpack.1 = (f32[2048,512]{1,0:T(8,128)}, f32[512,2048]{1,0:T(8,128)}, f32[512,1536]{1,0:T(8,128)}, f32[512,512]{1,0:T(8,128)}, f32[12,36,2,512]{3,2,1,0:T(2,128)}) custom-call(bf16[12,512,512]{2,1,0:T(8,128)(2,1)} %get-tuple-element.12.g_ref, f32[12,36,2,512]{3,2,1,0:T(2,128)} %get-tuple-element.13.tok_ref), custom_call_target="tpu_custom_call" | custom-call | tf_op jit(solution)/shard_map/unpack/pallas_call | solution.py:234

commit v6 on v5

--- a/solution.py
+++ b/solution.py
@@ -66,11 +66,14 @@
 IN_BLOCKS = (1, 3, 5, 7)
 PROJ_BLOCK = 8
 QKV_BLOCKS = (9, 10, 11)
-ROUTES = (
-    ("xyz", 1), ("yzx", 1), ("zxy", 1), ("xyz", 3), ("yzx", 3), ("zxy", 3),
-    ("xyz", 1), ("yzx", 1), ("zxy", 0),
-    ("xyz", 0), ("yzx", 0), ("zxy", 0),
+UNITS = (
+    (0, 0, D, "xyz", 1), (1, 0, D, "yzx", 1), (2, 0, D, "zxy", 1), (3, 0, D, "xyz", 3),
+    (4, 0, D, "yzx", 3), (5, 0, D, "zxy", 3), (6, 0, D, "xyz", 1), (7, 0, D, "yzx", 1),
+    (8, 0, D, "zxy", 0),
+    (9, 0, LANES, "xyz", 0), (10, 0, LANES, "yzx", 0), (11, 0, LANES, "zxy", 0),
+    (9, LANES, LANES, "xyz", 0), (10, LANES, LANES, "yzx", 0), (11, LANES, LANES, "zxy", 0),
 )
+QKV_UNITS = ((9, 10, 11), (12, 13, 14))
 SLOTS = 17
 
 
@@ -110,7 +113,8 @@
     def __init__(self, place, u, g, done, got, send, recv):
         self.u, self.g, self.done, self.got, self.send, self.recv = u, g, done, got, send, recv
         self.stage, self.slots, self.copies = 0, 0, []
-        order, first = ROUTES[u]
+        self.block, col, width, order, first = UNITS[u]
+        self.cols = pl.ds(col, width)
         self.steps, base, rows = [], 0, D
 
         def halve(name, target, bit, base, rows):
@@ -136,7 +140,7 @@
         self.last = 2 * len(self.steps) + 1
 
     def part(self, ref, base, rows):
-        return ref.at[self.u, pl.ds(pl.multiple_of(base, rows), rows), :]
+        return ref.at[self.block, pl.ds(pl.multiple_of(base, rows), rows), self.cols]
 
     def copy(self, src, dst, target):
         slot = self.slots
@@ -150,8 +154,8 @@
 
     def landing(self, name, i):
         if name == "axis":
-            return self.got[name].at[i, self.u - PROJ_BLOCK]
-        return self.got[name].at[i, self.u]
+            return self.got[name].at[i, self.block - PROJ_BLOCK, :, self.cols]
+        return self.got[name].at[i, self.block, :, self.cols]
 
     def advance(self):
         n, stage = len(self.steps), self.stage
@@ -168,7 +172,7 @@
             mine[...] = total.astype(BF16)
         if stage == n + 1:
             _, _, base, rows = self.swap
-            four = [self.got["swap"][c, self.u].astype(F32) for c in range(4)]
+            four = [self.got["swap"][c, self.block, :, self.cols].astype(F32) for c in range(4)]
             self.part(self.done, base, rows)[...] = ((four[0] + four[1]) + (four[2] + four[3])).astype(BF16)
         if stage < n:
             name, targets, _, rows = self.steps[stage]
@@ -177,9 +181,9 @@
         elif stage == n:
             targets, at, base, rows = self.swap
             mine = self.part(self.g, base, rows)
-            self.got["swap"][at, self.u] = mine[...]
+            self.got["swap"][at, self.block, :, self.cols] = mine[...]
             for target in targets:
-                self.copy(mine, self.got["swap"].at[at, self.u], target)
+                self.copy(mine, self.got["swap"].at[at, self.block, :, self.cols], target)
         elif stage <= 2 * n:
             _, targets, base, rows = self.steps[2 * n - stage]
             mine = self.part(self.done, base, rows)
@@ -198,7 +202,7 @@
 
 
 def sum_scratch():
-    return [pltpu.VMEM(shape, BF16) for _, shape in LANDINGS] + [pltpu.SemaphoreType.DMA((BLOCKS, SLOTS))] * 2
+    return [pltpu.VMEM(shape, BF16) for _, shape in LANDINGS] + [pltpu.SemaphoreType.DMA((len(UNITS), SLOTS))] * 2
 
 
 def unpack_kernel(g_ref, tok_ref, out_ref, in_ref, qkv_ref, proj_ref, tok_out, half, full, lines_in, got, put, whole):
@@ -359,10 +363,13 @@
 
 AFTER_CHUNK = ((0, 1), (0, 1, 2, 3), (2, 3, 4, 5), (0, 1, 4, 5, 6, 7))
 AFTER_PROJ = (8, 0, 1, 2, 3, 6, 7)
-AFTER_WINDOW = ((4, 5), (0, 1, 2, 3, 8), (4, 5, 6, 7), (0, 1, 2, 3), (4, 5, 6, 7, 8), (0, 1, 2, 3))
+AFTER_WINDOW = (
+    ((), (4, 5), (), (0, 1, 2, 3, 8), (), (4, 5, 6, 7)),
+    ((), (0, 1, 2, 3, 9, 10, 11), (), (4, 5, 6, 7, 8), (), (0, 1, 2, 3, 9, 10, 11)),
+)
 AFTER_QKV = (4, 5, 6, 7, 8)
-AFTER_INPUT = (9, 10, 11, 0, 1, 2, 3)
-AFTER_NORM = (4, 5, 6, 7, 8)
+AFTER_INPUT = (12, 13, 14, 9, 10, 11, 0, 1, 2, 3)
+AFTER_NORM = (9, 10, 11, 4, 5, 6, 7, 8)
 
 
 def block_kernel(
@@ -375,9 +382,14 @@
     place = Place()
     *landings, send, recv = landings_and_sems
     got = {name: ref for (name, _), ref in zip(LANDINGS, landings)}
-    sums = [Sum(place, u, g_ref, done_ref, got, send, recv) for u in range(BLOCKS)]
-
-    leaving = {u: pltpu.make_async_copy(done_ref.at[u], done_hbm.at[u], done_sem.at[u]) for u in range(BLOCKS)}
+    sums = [Sum(place, u, g_ref, done_ref, got, send, recv) for u in range(len(UNITS))]
+
+    leaving = [
+        pltpu.make_async_copy(
+            done_ref.at[one.block, :, one.cols], done_hbm.at[one.block, :, one.cols], done_sem.at[one.u]
+        )
+        for one in sums
+    ]
 
     def tick(*blocks):
         for u in blocks:
@@ -512,13 +524,14 @@
     tick(*AFTER_PROJ)
     mixed[...] = nt(nmid[...], wproj_ref[...]).astype(BF16)
 
-    for w in range(WINDOWS):
-
-        @pl.loop(w, w + 1)
-        def _(w):
-            rows = rows_of(w)
-            for g in range(GROUPS):
-                lo = LANES * g
+    normed_t = normed[...].T
+    for g in range(GROUPS):
+        lo = LANES * g
+        for w in range(WINDOWS):
+
+            @pl.loop(w, w + 1)
+            def _(w):
+                rows = rows_of(w)
                 q = spread_heads(packed[rows, lo : lo + LANES])
                 k = packed[rows, D + lo : D + lo + LANES]
                 v = packed[rows, 2 * D + lo : 2 * D + lo + LANES]
@@ -532,12 +545,12 @@
                 packed[rows, D + lo : D + lo + LANES] = nn(ds, q).astype(BF16)
                 packed[rows, 2 * D + lo : 2 * D + lo + LANES] = nn(p, do).astype(BF16)
 
-        tick(*AFTER_WINDOW[w])
-
-    normed_t = normed[...].T
-    for j in range(3):
-        g_ref[QKV_BLOCKS[j]] = nn(normed_t, packed[:, D * j : D * (j + 1)]).astype(BF16)
-        tick(QKV_BLOCKS[j])
+            tick(*AFTER_WINDOW[g][w])
+        for j in range(3):
+            g_ref[QKV_BLOCKS[j], :, lo : lo + LANES] = nn(
+                normed_t, packed[:, D * j + lo : D * j + lo + LANES]
+            ).astype(BF16)
+            tick(QKV_UNITS[g][j])
     tick(*AFTER_QKV)
     for j in range(3):
         cols = slice(D * j, D * (j + 1))
@@ -561,13 +574,13 @@
 
     rounds = 0
     while any(one.stage <= one.last for one in sums):
-        tick(*(u for u in (9, 10, 11, 0, 1, 2, 3, 4, 5, 6, 7, 8) if sums[u].stage <= sums[u].last))
+        tick(*(u for u in (*QKV_UNITS[1], *QKV_UNITS[0], 0, 1, 2, 3, 4, 5, 6, 7, 8) if sums[u].stage <= sums[u].last))
         rounds += 1
         if rounds == 2:
             for one in grad_halo:
                 one.wait()
             return_halo(back_in, out_ref)
-    for one in leaving.values():
+    for one in leaving:
         one.wait()
 
 
@@ -603,7 +616,7 @@
             pltpu.VMEM((HALO_ROWS, D), BF16),
             pltpu.SemaphoreType.DMA((6,)),
             pltpu.SemaphoreType.DMA((2, 9)),
-            pltpu.SemaphoreType.DMA((BLOCKS,)),
+            pltpu.SemaphoreType.DMA((len(UNITS),)),
         ]
         + sum_scratch(),
         compiler_params=pltpu.CompilerParams(

time: 110 us -> 115 us (1.045)
  Pallas kernels: 109 us -> 114 us
    pallas_call x1, Pallas kernels: 101 us -> 105 us  [block_call(): pl.pallas_call(block_kernel, out_shape=(jax.ShapeDtypeStruct(tokens.shape...]
where the time goes in v6:
time: 115 us
  Pallas kernels  114 us (99%)
    pallas_call x1, Pallas kernels, block_call(): pl.pallas_call(block_kernel, out_shape=(jax.ShapeDtypeStruct(tokens.shape...  105 us
    pallas_call x1, Pallas kernels, unpack_call(): pl.pallas_call(unpack_kernel, out_shape=tuple((jax.ShapeDtypeStruct(s, F3...  8.57 us

profile of v6, /device:TPU:1, one launch (start us, length us, event | category | flops | bytes accessed | tf_op | source)
XLA Modules:
  0.0 114.6 jit_solution(10359484256974705819)
XLA Ops:
  0.6 105.1 %block.1 = (f32[12,36,2,512]{3,2,1,0:T(2,128)}, bf16[12,512,512]{2,1,0:T(8,128)(2,1)}) custom-call(f32[12,36,2,512]{3,2,1,0:T(2,128)} %bitcast.4, f32[12,36,2,512]{3,2,1,0:T(2,128)} %bitcast.5, s32[12,2,36]{2,1,0:T(2,128)} %bitcast.7, bf16[512,1536]{1,0:T(8,128)(2,1)} %wqkv.1, bf16[512,512]{1,0:T(8,128)(2,1)} %wproj.1, bf16[512,2048]{1,0:T(8,128)(2,1)} %win.1, ...), custom_call_target="tpu_custom_call" | custom-call | flops 16000000000 | bytes 24000000 | tf_op jit(solution)/shard_map/block/pallas_call | solution.py:590
  105.8 8.6 %unpack.1 = (f32[2048,512]{1,0:T(8,128)}, f32[512,2048]{1,0:T(8,128)}, f32[512,1536]{1,0:T(8,128)}, f32[512,512]{1,0:T(8,128)}, f32[12,36,2,512]{3,2,1,0:T(2,128)}) custom-call(bf16[12,512,512]{2,1,0:T(8,128)(2,1)} %get-tuple-element.12.g_ref, f32[12,36,2,512]{3,2,1,0:T(2,128)} %get-tuple-element.13.tok_ref), custom_call_target="tpu_custom_call" | custom-call | tf_op jit(solution)/shard_map/unpack/pallas_call | solution.py:238

commit v7 on v5

--- a/solution.py
+++ b/solution.py
@@ -66,12 +66,14 @@
 IN_BLOCKS = (1, 3, 5, 7)
 PROJ_BLOCK = 8
 QKV_BLOCKS = (9, 10, 11)
-ROUTES = (
-    ("xyz", 1), ("yzx", 1), ("zxy", 1), ("xyz", 3), ("yzx", 3), ("zxy", 3),
-    ("xyz", 1), ("yzx", 1), ("zxy", 0),
-    ("xyz", 0), ("yzx", 0), ("zxy", 0),
+UNITS = (
+    (0, 2, "xyz"), (2, 2, "yzx"), (4, 2, "zxy"), (6, 2, "xyz"),
+    (8, 1, "yzx"), (9, 1, "xyz"), (10, 1, "yzx"), (11, 1, "zxy"),
 )
-SLOTS = 17
+QKV_UNITS = (5, 6, 7)
+PAIRED = 8
+SLOTS = 19
+SPLIT = (4, 2, D // 8, D)
 
 
 class Place:
@@ -108,35 +110,59 @@
 
 class Sum:
     def __init__(self, place, u, g, done, got, send, recv):
-        self.u, self.g, self.done, self.got, self.send, self.recv = u, g, done, got, send, recv
+        first, count, order = UNITS[u]
+        self.u, self.g, self.done, self.send, self.recv = u, g, done, send, recv
+        self.blocks = blocks = pl.ds(first, count)
         self.stage, self.slots, self.copies = 0, 0, []
-        order, first = ROUTES[u]
-        self.steps, base, rows = [], 0, D
-
-        def halve(name, target, bit, base, rows):
-            rows //= 2
-            self.steps.append((name, [(target, base + (1 - bit) * rows)], base + bit * rows, rows))
-            return base + bit * rows, rows
-
-        def quarter(name, axis, base, rows):
-            rows //= 4
+        top, other = place.core * 2, (1 - place.core) * 2
+        self.steps = []
+
+        def half(pieces):
+            self.steps.append((
+                [(out, land, target) for out, keep, land, target in pieces],
+                [(keep, [land]) for out, keep, land, target in pieces],
+                [(keep, target) for out, keep, land, target in pieces],
+            ))
+
+        def quarter(axis, piece, landing):
             peers = [place.along(axis, step) for step in (1, 2, 3)]
-            self.steps.append((name, [(t, base + c * rows) for t, c in peers], base + place.at[axis] * rows, rows))
-            return base + place.at[axis] * rows, rows
-
-        base, rows = halve("core", place.sibling(), place.core, base, rows)
-        if first:
-            base, rows = halve("near", *place.across(order[0], first), base, rows)
-            base, rows = halve("far", *place.across(order[0], 4 - first), base, rows)
+            keep = piece(place.at[axis])
+            self.steps.append((
+                [(piece(c), landing[i], target) for i, (target, c) in enumerate(peers)],
+                [(keep, landing)],
+                [(keep, target) for target, _ in peers],
+            ))
+
+        half([(
+            lambda r: r.at[blocks, pl.ds(other, 2)], lambda r: r.at[blocks, pl.ds(top, 2)],
+            got["core"].at[blocks], place.sibling(),
+        )])
+        if count == 2:
+            a, b = first, first + 1
+            (one, h1), (three, h3) = place.across(order[0], 1), place.across(order[0], 3)
+            near, far = got["near"], got["far"]
+            half([
+                (lambda r: r.at[a, top + 1 - h1], lambda r: r.at[a, top + h1], near.at[a], one),
+                (lambda r: r.at[b, pl.ds(top, 2), 1 - h3], lambda r: r.at[b, pl.ds(top, 2), h3], near.at[b], three),
+            ])
+            half([
+                (lambda r: r.at[a, top + h1, 1 - h3], lambda r: r.at[a, top + h1, h3], far.at[a], three),
+                (lambda r: r.at[b, top + 1 - h1, h3], lambda r: r.at[b, top + h1, h3], far.at[b], one),
+            ])
+            at1, at3 = top + h1, h3
         else:
-            base, rows = quarter("axis", order[0], base, rows)
-        base, rows = quarter("second", order[1], base, rows)
+            land = [got["axis"].at[i, pl.ds(first - PAIRED, count)] for i in range(3)]
+            quarter(order[0], lambda c: lambda r: r.at[blocks, top + c // 2, c % 2], land)
+            c = place.at[order[0]]
+            at1, at3 = top + c // 2, c % 2
+
+        def small(c):
+            return lambda r: r.at[blocks, at1, at3, pl.ds(pl.multiple_of(c * (D // 32), D // 32), D // 32)]
+
+        quarter(order[1], small, [got["second"].at[i, blocks] for i in range(3)])
         peers = [place.along(order[2], step)[0] for step in (1, 2, 3)]
-        self.swap = (peers, place.at[order[2]], base, rows)
+        self.swap = (peers, small(place.at[order[1]]), place.at[order[2]], got["swap"])
         self.last = 2 * len(self.steps) + 1
-
-    def part(self, ref, base, rows):
-        return ref.at[self.u, pl.ds(pl.multiple_of(base, rows), rows), :]
 
     def copy(self, src, dst, target):
         slot = self.slots
@@ -148,57 +174,48 @@
         one.start()
         self.copies.append(one)
 
-    def landing(self, name, i):
-        if name == "axis":
-            return self.got[name].at[i, self.u - PROJ_BLOCK]
-        return self.got[name].at[i, self.u]
-
     def advance(self):
         n, stage = len(self.steps), self.stage
         self.stage += 1
         for one in self.copies:
             one.wait()
         self.copies = []
+        peers, piece, at, slots = self.swap
         if 1 <= stage <= n:
-            name, targets, base, rows = self.steps[stage - 1]
-            mine = self.part(self.g, base, rows)
-            total = mine[...].astype(F32)
-            for i in range(len(targets)):
-                total = total + self.landing(name, i)[...].astype(F32)
-            mine[...] = total.astype(BF16)
+            for keep, landings in self.steps[stage - 1][1]:
+                mine = keep(self.g)
+                total = mine[...].astype(F32)
+                for landing in landings:
+                    total = total + landing[...].astype(F32)
+                mine[...] = total.astype(BF16)
         if stage == n + 1:
-            _, _, base, rows = self.swap
-            four = [self.got["swap"][c, self.u].astype(F32) for c in range(4)]
-            self.part(self.done, base, rows)[...] = ((four[0] + four[1]) + (four[2] + four[3])).astype(BF16)
+            four = [slots[c, self.blocks].astype(F32) for c in range(4)]
+            piece(self.done)[...] = ((four[0] + four[1]) + (four[2] + four[3])).astype(BF16)
         if stage < n:
-            name, targets, _, rows = self.steps[stage]
-            for i, (target, base) in enumerate(targets):
-                self.copy(self.part(self.g, base, rows), self.landing(name, i), target)
+            for out, landing, target in self.steps[stage][0]:
+                self.copy(out(self.g), landing, target)
         elif stage == n:
-            targets, at, base, rows = self.swap
-            mine = self.part(self.g, base, rows)
-            self.got["swap"][at, self.u] = mine[...]
-            for target in targets:
-                self.copy(mine, self.got["swap"].at[at, self.u], target)
+            mine = piece(self.g)
+            slots[at, self.blocks] = mine[...]
+            for target in peers:
+                self.copy(mine, slots.at[at, self.blocks], target)
         elif stage <= 2 * n:
-            _, targets, base, rows = self.steps[2 * n - stage]
-            mine = self.part(self.done, base, rows)
-            for target, _ in targets:
-                self.copy(mine, mine, target)
+            for keep, target in self.steps[2 * n - stage][2]:
+                self.copy(keep(self.done), keep(self.done), target)
 
 
 LANDINGS = (
-    ("core", (1, BLOCKS, D // 2, D)),
-    ("near", (1, BLOCKS - 3, D // 4, D)),
-    ("far", (1, BLOCKS - 3, D // 8, D)),
-    ("axis", (3, 4, D // 8, D)),
+    ("core", (BLOCKS, 2, 2, D // 8, D)),
+    ("near", (PAIRED, 2, D // 8, D)),
+    ("far", (PAIRED, D // 8, D)),
+    ("axis", (3, BLOCKS - PAIRED, D // 8, D)),
     ("second", (3, BLOCKS, D // 32, D)),
     ("swap", (4, BLOCKS, D // 32, D)),
 )
 
 
 def sum_scratch():
-    return [pltpu.VMEM(shape, BF16) for _, shape in LANDINGS] + [pltpu.SemaphoreType.DMA((BLOCKS, SLOTS))] * 2
+    return [pltpu.VMEM(shape, BF16) for _, shape in LANDINGS] + [pltpu.SemaphoreType.DMA((len(UNITS), SLOTS))] * 2
 
 
 def unpack_kernel(g_ref, tok_ref, out_ref, in_ref, qkv_ref, proj_ref, tok_out, half, full, lines_in, got, put, whole):
@@ -357,12 +374,12 @@
             flat[cell(row, wide) : cell(row, wide) + LINE, :] = both[LINE * wide : LINE * (wide + 1)]
 
 
-AFTER_CHUNK = ((0, 1), (0, 1, 2, 3), (2, 3, 4, 5), (0, 1, 4, 5, 6, 7))
-AFTER_PROJ = (8, 0, 1, 2, 3, 6, 7)
-AFTER_WINDOW = ((4, 5), (0, 1, 2, 3, 8), (4, 5, 6, 7), (0, 1, 2, 3), (4, 5, 6, 7, 8), (0, 1, 2, 3))
-AFTER_QKV = (4, 5, 6, 7, 8)
-AFTER_INPUT = (9, 10, 11, 0, 1, 2, 3)
-AFTER_NORM = (4, 5, 6, 7, 8)
+AFTER_CHUNK = ((0,), (1,), (0, 2), (1, 3))
+AFTER_PROJ = (4, 0, 2)
+AFTER_WINDOW = ((1, 3), (4,), (0, 2), (1, 3), (4,), (0, 2))
+AFTER_QKV = (1, 3, 4)
+AFTER_INPUT = (5, 6, 7, 0, 2)
+AFTER_NORM = (1, 3, 4)
 
 
 def block_kernel(
@@ -375,9 +392,11 @@
     place = Place()
     *landings, send, recv = landings_and_sems
     got = {name: ref for (name, _), ref in zip(LANDINGS, landings)}
-    sums = [Sum(place, u, g_ref, done_ref, got, send, recv) for u in range(BLOCKS)]
-
-    leaving = {u: pltpu.make_async_copy(done_ref.at[u], done_hbm.at[u], done_sem.at[u]) for u in range(BLOCKS)}
+    sums = [Sum(place, u, g_ref, done_ref, got, send, recv) for u in range(len(UNITS))]
+
+    leaving = [
+        pltpu.make_async_copy(done_ref.at[one.blocks], done_hbm.at[one.blocks], done_sem.at[one.u]) for one in sums
+    ]
 
     def tick(*blocks):
         for u in blocks:
@@ -491,8 +510,8 @@
         act = (u * half).astype(BF16)
         slope = half + u * (0.5 - 0.5 * t * t) * (GELU_A + (3 * GELU_A * GELU_B) * square)
         dpre = (slope * da).astype(BF16)
-        g_ref[OUT_BLOCKS[j]] = nn(act.T, cot).astype(BF16)
-        g_ref[IN_BLOCKS[j]] = nn(nmid_t, dpre).astype(BF16)
+        g_ref[OUT_BLOCKS[j]] = nn(act.T, cot).astype(BF16).reshape(SPLIT)
+        g_ref[IN_BLOCKS[j]] = nn(nmid_t, dpre).astype(BF16).reshape(SPLIT)
         part = nt(dpre, win_ref[:, cols])
         if j == 0:
             dnm[...] = part
@@ -508,7 +527,7 @@
         c_ref[rows, :] = d_mid
         nmid[rows, :] = d_mid.astype(BF16)
 
-    g_ref[PROJ_BLOCK] = nn(mixed[...].T, nmid[...]).astype(BF16)
+    g_ref[PROJ_BLOCK] = nn(mixed[...].T, nmid[...]).astype(BF16).reshape(SPLIT)
     tick(*AFTER_PROJ)
     mixed[...] = nt(nmid[...], wproj_ref[...]).astype(BF16)
 
@@ -536,8 +555,8 @@
 
     normed_t = normed[...].T
     for j in range(3):
-        g_ref[QKV_BLOCKS[j]] = nn(normed_t, packed[:, D * j : D * (j + 1)]).astype(BF16)
-        tick(QKV_BLOCKS[j])
+        g_ref[QKV_BLOCKS[j]] = nn(normed_t, packed[:, D * j : D * (j + 1)]).astype(BF16).reshape(SPLIT)
+        tick(QKV_UNITS[j])
     tick(*AFTER_QKV)
     for j in range(3):
         cols = slice(D * j, D * (j + 1))
@@ -561,13 +580,13 @@
 
     rounds = 0
     while any(one.stage <= one.last for one in sums):
-        tick(*(u for u in (9, 10, 11, 0, 1, 2, 3, 4, 5, 6, 7, 8) if sums[u].stage <= sums[u].last))
+        tick(*(u for u in (*QKV_UNITS, 0, 1, 2, 3, 4) if sums[u].stage <= sums[u].last))
         rounds += 1
         if rounds == 2:
             for one in grad_halo:
                 one.wait()
             return_halo(back_in, out_ref)
-    for one in leaving.values():
+    for one in leaving:
         one.wait()
 
 
@@ -576,11 +595,11 @@
     count = WINDOWS * WIN
     return pl.pallas_call(
         block_kernel,
-        out_shape=(jax.ShapeDtypeStruct(tokens.shape, F32), jax.ShapeDtypeStruct((BLOCKS, D, D), BF16)),
+        out_shape=(jax.ShapeDtypeStruct(tokens.shape, F32), jax.ShapeDtypeStruct((BLOCKS, *SPLIT), BF16)),
         in_specs=[anywhere, anywhere, vmem] + [anywhere] * 4,
         out_specs=(vmem, anywhere),
         scratch_shapes=[
-            pltpu.VMEM((BLOCKS, D, D), BF16),
+            pltpu.VMEM((BLOCKS, *SPLIT), BF16),
             pltpu.VMEM(tokens.shape, F32),
             pltpu.VMEM((count, 128), F32),
             pltpu.VMEM((count, D), F32),
@@ -596,14 +615,14 @@
             pltpu.VMEM((count, D), F32),
             pltpu.VMEM((count, D), BF16),
             pltpu.VMEM((count, D), F32),
-            pltpu.VMEM((BLOCKS, D, D), BF16),
+            pltpu.VMEM((BLOCKS, *SPLIT), BF16),
             pltpu.VMEM((2, HALO_ROWS, D), BF16),
             pltpu.VMEM((2, HALO_ROWS, D), BF16),
             pltpu.VMEM((HALO_ROWS, D), BF16),
             pltpu.VMEM((HALO_ROWS, D), BF16),
             pltpu.SemaphoreType.DMA((6,)),
             pltpu.SemaphoreType.DMA((2, 9)),
-            pltpu.SemaphoreType.DMA((BLOCKS,)),
+            pltpu.SemaphoreType.DMA((len(UNITS),)),
         ]
         + sum_scratch(),
         compiler_params=pltpu.CompilerParams(
@@ -619,7 +638,7 @@
         tokens.transpose(1, 2, 0, 3), cotangent.transpose(1, 2, 0, 3), region_ids.transpose(1, 0, 2),
         w_qkv, w_proj, w_in, w_out,
     )
-    grad_out, grad_in, grad_qkv, grad_proj, grad_tokens = unpack_call(grads, grad_tokens)
+    grad_out, grad_in, grad_qkv, grad_proj, grad_tokens = unpack_call(grads.reshape(BLOCKS, D, D), grad_tokens)
     return grad_tokens.transpose(2, 0, 1, 3), grad_qkv, grad_proj, grad_in, grad_out
 
 

time: 110 us -> 106 us (0.964)
  Pallas kernels: 109 us -> 105 us
    pallas_call x1, Pallas kernels: 101 us -> 96.5 us  [block_call(): pl.pallas_call(block_kernel, out_shape=(jax.ShapeDtypeStruct(tokens.shape...]
where the time goes in v7:
time: 106 us
  Pallas kernels  105 us (99%)
    pallas_call x1, Pallas kernels, block_call(): pl.pallas_call(block_kernel, out_shape=(jax.ShapeDtypeStruct(tokens.shape...  96.5 us
    pallas_call x1, Pallas kernels, unpack_call(): pl.pallas_call(unpack_kernel, out_shape=tuple((jax.ShapeDtypeStruct(s, F3...  8.57 us

profile of v7, /device:TPU:1, one launch (start us, length us, event | category | flops | bytes accessed | tf_op | source)
XLA Modules:
  0.0 105.9 jit_solution(235442859513081397)
XLA Ops:
  0.6 96.5 %block.1 = (f32[12,36,2,512]{3,2,1,0:T(2,128)}, bf16[12,4,2,64,512]{4,3,2,1,0:T(8,128)(2,1)}) custom-call(f32[12,36,2,512]{3,2,1,0:T(2,128)} %bitcast.6, f32[12,36,2,512]{3,2,1,0:T(2,128)} %bitcast.7, s32[12,2,36]{2,1,0:T(2,128)} %bitcast.9, bf16[512,1536]{1,0:T(8,128)(2,1)} %wqkv.1, bf16[512,512]{1,0:T(8,128)(2,1)} %wproj.1, bf16[512,2048]{1,0:T(8,128)(2,1)} %win.1, ...), custom_call_target="tpu_custom_call" | custom-call | flops 16000000000 | bytes 24000000 | tf_op jit(solution)/shard_map/block/pallas_call | solution.py:596
  97.1 8.6 %unpack.1 = (f32[2048,512]{1,0:T(8,128)}, f32[512,2048]{1,0:T(8,128)}, f32[512,1536]{1,0:T(8,128)}, f32[512,512]{1,0:T(8,128)}, f32[12,36,2,512]{3,2,1,0:T(2,128)}) custom-call(bf16[12,512,512]{2,1,0:T(8,128)(2,1)} %bitcast.5, f32[12,36,2,512]{3,2,1,0:T(2,128)} %get-tuple-element.13.tok_ref), custom_call_target="tpu_custom_call" | custom-call | tf_op jit(solution)/shard_map/unpack/pallas_call | solution.py:251

commit v8 on v7

--- a/solution.py
+++ b/solution.py
@@ -67,12 +67,12 @@
 PROJ_BLOCK = 8
 QKV_BLOCKS = (9, 10, 11)
 UNITS = (
-    (0, 2, "xyz"), (2, 2, "yzx"), (4, 2, "zxy"), (6, 2, "xyz"),
-    (8, 1, "yzx"), (9, 1, "xyz"), (10, 1, "yzx"), (11, 1, "zxy"),
+    (0, 2, "xyz"), (2, 2, "yzx"), (4, 2, "zxy"), (6, 3, "xyz"),
+    (9, 1, "xyz"), (10, 1, "yzx"), (11, 1, "zxy"),
 )
-QKV_UNITS = (5, 6, 7)
-PAIRED = 8
-SLOTS = 19
+QKV_UNITS = (4, 5, 6)
+PAIRED = 9
+SLOTS = 23
 SPLIT = (4, 2, D // 8, D)
 
 
@@ -137,18 +137,24 @@
             lambda r: r.at[blocks, pl.ds(other, 2)], lambda r: r.at[blocks, pl.ds(top, 2)],
             got["core"].at[blocks], place.sibling(),
         )])
-        if count == 2:
-            a, b = first, first + 1
+        if count > 1:
             (one, h1), (three, h3) = place.across(order[0], 1), place.across(order[0], 3)
             near, far = got["near"], got["far"]
-            half([
-                (lambda r: r.at[a, top + 1 - h1], lambda r: r.at[a, top + h1], near.at[a], one),
-                (lambda r: r.at[b, pl.ds(top, 2), 1 - h3], lambda r: r.at[b, pl.ds(top, 2), h3], near.at[b], three),
-            ])
-            half([
-                (lambda r: r.at[a, top + h1, 1 - h3], lambda r: r.at[a, top + h1, h3], far.at[a], three),
-                (lambda r: r.at[b, top + 1 - h1, h3], lambda r: r.at[b, top + h1, h3], far.at[b], one),
-            ])
+
+            def near_one(u):
+                return lambda r: r.at[u, top + 1 - h1], lambda r: r.at[u, top + h1], near.at[u], one
+
+            def near_three(u):
+                return lambda r: r.at[u, pl.ds(top, 2), 1 - h3], lambda r: r.at[u, pl.ds(top, 2), h3], near.at[u], three
+
+            def far_three(u):
+                return lambda r: r.at[u, top + h1, 1 - h3], lambda r: r.at[u, top + h1, h3], far.at[u], three
+
+            def far_one(u):
+                return lambda r: r.at[u, top + 1 - h1, h3], lambda r: r.at[u, top + h1, h3], far.at[u], one
+
+            half([(near_three if i == 1 else near_one)(first + i) for i in range(count)])
+            half([(far_one if i == 1 else far_three)(first + i) for i in range(count)])
             at1, at3 = top + h1, h3
         else:
             land = [got["axis"].at[i, pl.ds(first - PAIRED, count)] for i in range(3)]
@@ -374,12 +380,12 @@
             flat[cell(row, wide) : cell(row, wide) + LINE, :] = both[LINE * wide : LINE * (wide + 1)]
 
 
-AFTER_CHUNK = ((0,), (1,), (0, 2), (1, 3))
-AFTER_PROJ = (4, 0, 2)
-AFTER_WINDOW = ((1, 3), (4,), (0, 2), (1, 3), (4,), (0, 2))
-AFTER_QKV = (1, 3, 4)
-AFTER_INPUT = (5, 6, 7, 0, 2)
-AFTER_NORM = (1, 3, 4)
+AFTER_CHUNK = ((0,), (1,), (0, 2), (1,))
+AFTER_PROJ = (3, 0, 2)
+AFTER_WINDOW = ((1,), (3,), (0, 2), (1,), (3,), (0, 2))
+AFTER_QKV = (1, 3)
+AFTER_INPUT = (4, 5, 6, 0, 2)
+AFTER_NORM = (1, 3)
 
 
 def block_kernel(
@@ -580,7 +586,7 @@
 
     rounds = 0
     while any(one.stage <= one.last for one in sums):
-        tick(*(u for u in (*QKV_UNITS, 0, 1, 2, 3, 4) if sums[u].stage <= sums[u].last))
+        tick(*(u for u in (*QKV_UNITS, 0, 1, 2, 3) if sums[u].stage <= sums[u].last))
         rounds += 1
         if rounds == 2:
             for one in grad_halo:

time: 106 us -> 111 us (1.047)
  Pallas kernels: 105 us -> 110 us
    pallas_call x1, Pallas kernels: 96.5 us -> 102 us  [block_call(): pl.pallas_call(block_kernel, out_shape=(jax.ShapeDtypeStruct(tokens.shape...]
where the time goes in v8:
time: 111 us
  Pallas kernels  110 us (99%)
    pallas_call x1, Pallas kernels, block_call(): pl.pallas_call(block_kernel, out_shape=(jax.ShapeDtypeStruct(tokens.shape...  102 us
    pallas_call x1, Pallas kernels, unpack_call(): pl.pallas_call(unpack_kernel, out_shape=tuple((jax.ShapeDtypeStruct(s, F3...  8.57 us

profile of v8, /device:TPU:1, one launch (start us, length us, event | category | flops | bytes accessed | tf_op | source)
XLA Modules:
  0.0 111.0 jit_solution(9978639812396500705)
XLA Ops:
  0.6 101.6 %block.1 = (f32[12,36,2,512]{3,2,1,0:T(2,128)}, bf16[12,4,2,64,512]{4,3,2,1,0:T(8,128)(2,1)}) custom-call(f32[12,36,2,512]{3,2,1,0:T(2,128)} %bitcast.6, f32[12,36,2,512]{3,2,1,0:T(2,128)} %bitcast.7, s32[12,2,36]{2,1,0:T(2,128)} %bitcast.9, bf16[512,1536]{1,0:T(8,128)(2,1)} %wqkv.1, bf16[512,512]{1,0:T(8,128)(2,1)} %wproj.1, bf16[512,2048]{1,0:T(8,128)(2,1)} %win.1, ...), custom_call_target="tpu_custom_call" | custom-call | flops 16000000000 | bytes 24000000 | tf_op jit(solution)/shard_map/block/pallas_call | solution.py:602
  102.2 8.6 %unpack.1 = (f32[2048,512]{1,0:T(8,128)}, f32[512,2048]{1,0:T(8,128)}, f32[512,1536]{1,0:T(8,128)}, f32[512,512]{1,0:T(8,128)}, f32[12,36,2,512]{3,2,1,0:T(2,128)}) custom-call(bf16[12,512,512]{2,1,0:T(8,128)(2,1)} %bitcast.5, f32[12,36,2,512]{3,2,1,0:T(2,128)} %get-tuple-element.13.tok_ref), custom_call_target="tpu_custom_call" | custom-call | tf_op jit(solution)/shard_map/unpack/pallas_call | solution.py:257
